TPU v7x, 128 devices: a whole 4x4x4 slice. The times are simulated.
128 devices in a mesh: dp: 32 (over z_lo, x, y), tensor: 4 (over z_hi, core).
Axes of the slice: x: 4, y: 4, z: 4 (z_hi: 2, z_lo: 2; z = z_hi * 2 + z_lo), core: 2. Of those that a mesh axis runs over, the one named last changes fastest.
Arguments:
- images: bfloat16 [12608, 768], P('dp'), may hold values from -6 to 6
- routes: int32 [12608, 2], P('dp'), may hold values from 0 to 31, all different within a row; in each aligned block of 394 rows (0 to 393, 394 to 787, ...) at most 37 rows name the same one
- cotangent: bfloat16 [12608, 768], P('dp'), may hold values from -6 to 6
- qkv_weight: bfloat16 [2, 768, 3, 768], P(None, None, None, 'tensor'), may hold values from -0.21875 to 0.21875
- out_weight: bfloat16 [2, 768, 768], P(None, 'tensor'), may hold values from -1.5 to 1.5
- qv_bias: float32 [2, 2, 768], P(None, None, 'tensor'), may hold values from -1.5 to 1.5
- out_bias: float32 [2, 768], replicated, may hold values from -1.5 to 1.5
- ln_gain: float32 [4, 768], replicated, may hold values from 0.5 to 1.5
- ln_bias: float32 [4, 768], replicated, may hold values from -1.5 to 1.5
- dense_in: bfloat16 [768, 3072], P(None, 'tensor'), may hold values from -0.21875 to 0.21875
- dense_out: bfloat16 [3072, 768], P('tensor'), may hold values from -0.109375 to 0.109375
- router: bfloat16 [768, 32], replicated, may hold values from -0.15625 to 0.15625
- expert_in: bfloat16 [32, 768, 3072], P('dp', None, 'tensor'), may hold values from -0.21875 to 0.21875
- expert_out: bfloat16 [32, 3072, 768], P('dp', 'tensor'), may hold values from -0.109375 to 0.109375
Outputs:
- output: bfloat16 [12608, 768], P('dp')
- input_grad: float32 [12608, 768], P('dp')
- qkv_weight_grad: float32 [2, 768, 3, 768], P(None, None, None, 'tensor')
- out_weight_grad: float32 [2, 768, 768], P(None, 'tensor')
- qv_bias_grad: float32 [2, 2, 768], P(None, None, 'tensor')
- out_bias_grad: float32 [2, 768], replicated
- ln_gain_grad: float32 [4, 768], replicated
- ln_bias_grad: float32 [4, 768], replicated
- dense_in_grad: float32 [768, 3072], P(None, 'tensor')
- dense_out_grad: float32 [3072, 768], P('tensor')
- router_grad: float32 [768, 32], replicated
- expert_in_grad: float32 [32, 768, 3072], P('dp', None, 'tensor')
- expert_out_grad: float32 [32, 3072, 768], P('dp', 'tensor')
Inputs may be any that keep to these rules, and one draw needn't show every extreme that they name: `routes`: each token names two different experts. Among the 394 tokens of one index of dp no expert is named by more than 37 tokens, a bound that some expert reaches in some index's tokens.
All inputs are finite; a program needn't handle non-finite values.
Results may differ from a plain program's by a relative error of at most 0.038.
Values may be sent and summed in bfloat16 or wider, within the bound.
A program may use at most 128 MiB of HBM per device.

v0:
```python
import jax
import jax.numpy as jnp
from jax import lax
from jax.sharding import PartitionSpec as P

HEAD = 64
SEQ = 197


epsilon = 1e-06
bfloat = jnp.bfloat16
single = jnp.float32


def norm_forward(inputs, gain_row, shift_row):
    average = jnp.mean(inputs, axis=-1, keepdims=True)
    centered = inputs - average
    variance = jnp.mean(centered * centered, axis=-1, keepdims=True)
    inverse = lax.rsqrt(variance + epsilon)
    normal = centered * inverse
    return (normal * gain_row + shift_row, normal, inverse)


def norm_backward(grad_out, normal, inverse, gain_row):
    scaled = grad_out * gain_row
    mean_one = jnp.mean(scaled, axis=-1, keepdims=True)
    mean_two = jnp.mean(scaled * normal, axis=-1, keepdims=True)
    grad_in = inverse * (scaled - mean_one - normal * mean_two)
    return (grad_in, jnp.sum(grad_out * normal, axis=0), jnp.sum(grad_out, axis=0))


def gelu_exact(inputs):
    return jax.nn.gelu(inputs, approximate=False)


def gelu_slope(inputs, grad_out):
    unused, pullback = jax.vjp(gelu_exact, inputs)
    return pullback(grad_out)[0]


def attend_forward(
    inputs, layer_index, qkv_weight, out_weight, qv_bias, out_bias, ln_gain, ln_bias
):
    normed, normal, inverse = norm_forward(
        inputs, ln_gain[2 * layer_index], ln_bias[2 * layer_index]
    )
    normed_low = normed.astype(bfloat)
    projected = jnp.einsum(
        "td,dcf->tcf", normed_low, qkv_weight[layer_index], preferred_element_type=single
    )
    tokens_here, local_width = (projected.shape[0], projected.shape[2])
    head_shape = (tokens_here // SEQ, SEQ, local_width // HEAD, HEAD)
    queries = (projected[:, 0] + qv_bias[layer_index, 0]).astype(bfloat).reshape(head_shape)
    key_rows = projected[:, 1].astype(bfloat).reshape(head_shape)
    value_rows = (projected[:, 2] + qv_bias[layer_index, 1]).astype(bfloat).reshape(head_shape)
    scores = jnp.einsum(
        "bqhd,bkhd->bhqk", queries, key_rows, preferred_element_type=single
    ) * HEAD ** (-0.5)
    largest = jnp.max(scores, axis=-1, keepdims=True)
    exponent = jnp.exp(scores - largest)
    totals = jnp.sum(exponent, axis=-1, keepdims=True)
    probs_low = (exponent / totals).astype(bfloat)
    log_total = largest + jnp.log(totals)
    context = jnp.einsum("bhqk,bkhd->bqhd", probs_low, value_rows, preferred_element_type=single)
    context = context.reshape(tokens_here, local_width).astype(bfloat)
    partial_out = jnp.dot(context, out_weight[layer_index], preferred_element_type=single)
    summed = lax.psum(partial_out.astype(jnp.bfloat16), "tensor").astype(jnp.float32)
    stored = (normal, inverse, normed_low, queries, key_rows, value_rows, log_total, context)
    return (inputs + summed + out_bias[layer_index], stored)


def attend_backward(grad_out, layer_index, stored, qkv_weight, out_weight, ln_gain):
    normal, inverse, normed_low, queries, key_rows, value_rows, log_total, context = stored
    tokens_here, local_width = context.shape
    grad_low = grad_out.astype(bfloat)
    out_bias_part = jnp.sum(grad_out, axis=0)
    out_weight_part = jnp.einsum("tf,td->fd", context, grad_low, preferred_element_type=single)
    grad_context = jnp.einsum(
        "td,fd->tf", grad_low, out_weight[layer_index], preferred_element_type=single
    )
    grad_context = grad_context.astype(bfloat).reshape(queries.shape)
    scale_factor = HEAD ** (-0.5)
    scores = (
        jnp.einsum("bqhd,bkhd->bhqk", queries, key_rows, preferred_element_type=single)
        * scale_factor
    )
    probs_again = jnp.exp(scores - log_total)
    grad_values = jnp.einsum(
        "bhqk,bqhd->bkhd", probs_again.astype(bfloat), grad_context, preferred_element_type=single
    )
    grad_probs = jnp.einsum(
        "bqhd,bkhd->bhqk", grad_context, value_rows, preferred_element_type=single
    )
    row_total = jnp.sum(probs_again * grad_probs, axis=-1, keepdims=True)
    grad_scores = (probs_again * (grad_probs - row_total)).astype(bfloat)
    grad_queries = (
        jnp.einsum("bhqk,bkhd->bqhd", grad_scores, key_rows, preferred_element_type=single)
        * scale_factor
    )
    grad_keys = (
        jnp.einsum("bhqk,bqhd->bkhd", grad_scores, queries, preferred_element_type=single)
        * scale_factor
    )
    stacked = jnp.stack(
        [
            grad_queries.reshape(tokens_here, local_width),
            grad_keys.reshape(tokens_here, local_width),
            grad_values.reshape(tokens_here, local_width),
        ],
        axis=1,
    ).astype(bfloat)
    bias_part = jnp.stack(
        [
            jnp.sum(stacked[:, 0].astype(single), axis=0),
            jnp.sum(stacked[:, 2].astype(single), axis=0),
        ]
    )
    qkv_part = jnp.einsum("td,tcf->dcf", normed_low, stacked, preferred_element_type=single)
    normed_part = jnp.einsum(
        "tcf,dcf->td", stacked, qkv_weight[layer_index], preferred_element_type=single
    )
    grad_normed = lax.psum(normed_part.astype(jnp.bfloat16), "tensor").astype(jnp.float32)
    grad_in, gain_part, shift_part = norm_backward(
        grad_normed, normal, inverse, ln_gain[2 * layer_index]
    )
    return (
        grad_out + grad_in,
        (qkv_part, out_weight_part, bias_part, out_bias_part, gain_part, shift_part),
    )


def dense_forward(inputs, dense_in, dense_out, ln_gain, ln_bias):
    normed, normal, inverse = norm_forward(inputs, ln_gain[1], ln_bias[1])
    normed_low = normed.astype(bfloat)
    pre_act = jnp.dot(normed_low, dense_in, preferred_element_type=single)
    activated = gelu_exact(pre_act).astype(bfloat)
    partial_out = jnp.dot(activated, dense_out, preferred_element_type=single)
    summed = lax.psum(partial_out.astype(jnp.bfloat16), "tensor").astype(jnp.float32)
    return (inputs + summed, (normal, inverse, normed_low, pre_act, activated))


def dense_backward(grad_out, stored, dense_in, dense_out, ln_gain):
    normal, inverse, normed_low, pre_act, activated = stored
    grad_low = grad_out.astype(bfloat)
    out_part = jnp.einsum("tf,td->fd", activated, grad_low, preferred_element_type=single)
    grad_act = jnp.einsum("td,fd->tf", grad_low, dense_out, preferred_element_type=single)
    grad_pre = gelu_slope(pre_act, grad_act).astype(bfloat)
    in_part = jnp.einsum("td,tf->df", normed_low, grad_pre, preferred_element_type=single)
    normed_part = jnp.einsum("tf,df->td", grad_pre, dense_in, preferred_element_type=single)
    grad_normed = lax.psum(normed_part.astype(jnp.bfloat16), "tensor").astype(jnp.float32)
    grad_in, gain_part, shift_part = norm_backward(grad_normed, normal, inverse, ln_gain[1])
    return (grad_out + grad_in, (in_part, out_part, gain_part, shift_part))


def moe_forward(inputs, routes, router, expert_in, expert_out, ln_gain, ln_bias):
    normed, normal, inverse = norm_forward(inputs, ln_gain[3], ln_bias[3])
    normed_low = normed.astype(bfloat)
    logits = jnp.dot(normed_low, router, preferred_element_type=single)
    chosen = jnp.take_along_axis(logits, routes, axis=1)
    gate_values = jax.nn.softmax(chosen, axis=1)
    tokens_here, feature_width = normed_low.shape
    expert_count = router.shape[1]
    capacity = max(2, (3 * tokens_here + expert_count - 1) // expert_count)
    one_hot = (routes[:, :, None] == jnp.arange(expert_count, dtype=jnp.int32)).astype(jnp.int32)
    running = jnp.cumsum(one_hot.reshape(tokens_here * 2, expert_count), axis=0).reshape(
        tokens_here, 2, expert_count
    )
    slot_index = routes * capacity + jnp.sum((running - 1) * one_hot, axis=-1)
    slot_ids = jnp.arange(expert_count * capacity, dtype=jnp.int32)
    dispatch_pair = (slot_ids[None, :, None] == slot_index.T[:, None, :]).astype(bfloat)
    gathered = jnp.dot(
        jnp.sum(dispatch_pair, axis=0), normed_low, preferred_element_type=single
    ).astype(bfloat)
    outgoing = gathered.reshape(expert_count, capacity, feature_width)
    arrived_rows = lax.all_to_all(outgoing, "dp", split_axis=0, concat_axis=0, tiled=True)
    sources = arrived_rows.shape[0]
    items = arrived_rows.shape[1]
    rows_flat = arrived_rows.reshape(sources * items, feature_width)
    pre_rows = jnp.dot(rows_flat, expert_in[0], preferred_element_type=single)
    act_rows = gelu_exact(pre_rows).astype(bfloat)
    partial_out = jnp.dot(act_rows, expert_out[0], preferred_element_type=single)
    back_rows = lax.all_to_all(
        partial_out.reshape(sources, items, feature_width).astype(jnp.bfloat16),
        "dp",
        split_axis=0,
        concat_axis=0,
        tiled=True,
    ).astype(jnp.float32)
    hidden_width = pre_rows.shape[1]
    pre_act = pre_rows.reshape(sources, items, hidden_width)
    activated = act_rows.reshape(sources, items, hidden_width)
    picked = jnp.take(back_rows.reshape(expert_count * capacity, feature_width), slot_index, axis=0)
    mixed_part = jnp.sum(gate_values[:, :, None] * picked, axis=1)
    mixed = lax.psum(mixed_part.astype(jnp.bfloat16), "tensor").astype(jnp.float32)
    stored = (
        normal,
        inverse,
        normed_low,
        gate_values,
        slot_index,
        dispatch_pair,
        arrived_rows,
        pre_act,
        activated,
        picked,
    )
    return (inputs + mixed, stored)


def moe_backward(grad_out, routes, stored, router, expert_in, expert_out, ln_gain):
    (
        normal,
        inverse,
        normed_low,
        gate_values,
        slot_index,
        dispatch_pair,
        arrived,
        pre_act,
        activated,
        picked,
    ) = stored
    expert_count, capacity, feature_width = arrived.shape
    scaled = (gate_values[:, :, None] * grad_out[:, None, :]).astype(bfloat)
    outgoing = jnp.einsum(
        "kst,tkd->sd", dispatch_pair, scaled, preferred_element_type=single
    ).astype(bfloat)
    gate_part = jnp.sum(picked * grad_out[:, None, :], axis=-1)
    arrived_grad = lax.all_to_all(
        outgoing.reshape(expert_count, capacity, feature_width),
        "dp",
        split_axis=0,
        concat_axis=0,
        tiled=True,
    )
    row_count = expert_count * capacity
    rows_grad = arrived_grad.reshape(row_count, feature_width)
    flat_rows = arrived.reshape(row_count, feature_width)
    flat_pre = pre_act.reshape(row_count, pre_act.shape[2])
    flat_act = activated.reshape(row_count, activated.shape[2])
    expert_out_part = jnp.einsum("sf,sd->fd", flat_act, rows_grad, preferred_element_type=single)
    grad_act = jnp.einsum("sd,fd->sf", rows_grad, expert_out[0], preferred_element_type=single)
    grad_pre = gelu_slope(flat_pre, grad_act).astype(bfloat)
    expert_in_part = jnp.einsum("sd,sf->df", flat_rows, grad_pre, preferred_element_type=single)
    rows_back = jnp.einsum("sf,df->sd", grad_pre, expert_in[0], preferred_element_type=single)
    returned = lax.all_to_all(
        rows_back.reshape(expert_count, capacity, feature_width).astype(jnp.bfloat16),
        "dp",
        split_axis=0,
        concat_axis=0,
        tiled=True,
    ).astype(jnp.float32)
    normed_part = jnp.sum(
        jnp.take(returned.reshape(row_count, feature_width), slot_index, axis=0), axis=1
    )
    grad_experts, grad_gates = (
        lax.psum(normed_part.astype(jnp.bfloat16), "tensor").astype(jnp.float32),
        lax.psum(gate_part.astype(jnp.bfloat16), "tensor").astype(jnp.float32),
    )
    grad_chosen = gate_values * (
        grad_gates - jnp.sum(gate_values * grad_gates, axis=1, keepdims=True)
    )
    one_hot = (routes[:, :, None] == jnp.arange(router.shape[1], dtype=jnp.int32)).astype(single)
    grad_logits = jnp.sum(one_hot * grad_chosen[:, :, None], axis=1).astype(bfloat)
    router_part = jnp.einsum("td,te->de", normed_low, grad_logits, preferred_element_type=single)
    grad_normed = grad_experts + jnp.einsum(
        "te,de->td", grad_logits, router, preferred_element_type=single
    )
    grad_in, gain_part, shift_part = norm_backward(grad_normed, normal, inverse, ln_gain[3])
    return (
        grad_out + grad_in,
        (router_part, expert_in_part[None], expert_out_part[None], gain_part, shift_part),
    )


def per_device(
    images,
    routes,
    cotangent,
    qkv_weight,
    out_weight,
    qv_bias,
    out_bias,
    ln_gain,
    ln_bias,
    dense_in,
    dense_out,
    router,
    expert_in,
    expert_out,
):
    start_rows = images.astype(single)
    section_one, stored_one = attend_forward(
        start_rows, 0, qkv_weight, out_weight, qv_bias, out_bias, ln_gain, ln_bias
    )
    section_two, stored_dense = dense_forward(section_one, dense_in, dense_out, ln_gain, ln_bias)
    section_three, stored_two = attend_forward(
        section_two, 1, qkv_weight, out_weight, qv_bias, out_bias, ln_gain, ln_bias
    )
    section_four, stored_moe = moe_forward(
        section_three, routes, router, expert_in, expert_out, ln_gain, ln_bias
    )
    output = section_four.astype(bfloat)
    grad_four = cotangent.astype(single)
    grad_three, moe_parts = moe_backward(
        grad_four, routes, stored_moe, router, expert_in, expert_out, ln_gain
    )
    router_grad, expert_in_grad, expert_out_grad, gain_three, shift_three = moe_parts
    grad_two, upper_parts = attend_backward(
        grad_three, 1, stored_two, qkv_weight, out_weight, ln_gain
    )
    qkv_upper, outw_upper, bias_upper, outb_upper, gain_two, shift_two = upper_parts
    grad_one, dense_parts = dense_backward(grad_two, stored_dense, dense_in, dense_out, ln_gain)
    dense_in_grad, dense_out_grad, gain_one, shift_one = dense_parts
    input_grad, lower_parts = attend_backward(
        grad_one, 0, stored_one, qkv_weight, out_weight, ln_gain
    )
    qkv_lower, outw_lower, bias_lower, outb_lower, gain_zero, shift_zero = lower_parts
    (
        qkv_upper,
        outw_upper,
        bias_upper,
        outb_upper,
        gain_two,
        shift_two,
        router_grad,
        gain_three,
        shift_three,
        qkv_lower,
        outw_lower,
        bias_lower,
        outb_lower,
        gain_zero,
        shift_zero,
        gain_one,
        shift_one,
        dense_in_grad,
        dense_out_grad,
    ) = (
        lax.psum(qkv_upper.astype(jnp.bfloat16), "dp").astype(jnp.float32),
        lax.psum(outw_upper.astype(jnp.bfloat16), "dp").astype(jnp.float32),
        lax.psum(bias_upper.astype(jnp.bfloat16), "dp").astype(jnp.float32),
        lax.psum(outb_upper.astype(jnp.bfloat16), "dp").astype(jnp.float32),
        lax.psum(gain_two.astype(jnp.bfloat16), "dp").astype(jnp.float32),
        lax.psum(shift_two.astype(jnp.bfloat16), "dp").astype(jnp.float32),
        lax.psum(router_grad.astype(jnp.bfloat16), "dp").astype(jnp.float32),
        lax.psum(gain_three.astype(jnp.bfloat16), "dp").astype(jnp.float32),
        lax.psum(shift_three.astype(jnp.bfloat16), "dp").astype(jnp.float32),
        lax.psum(qkv_lower.astype(jnp.bfloat16), "dp").astype(jnp.float32),
        lax.psum(outw_lower.astype(jnp.bfloat16), "dp").astype(jnp.float32),
        lax.psum(bias_lower.astype(jnp.bfloat16), "dp").astype(jnp.float32),
        lax.psum(outb_lower.astype(jnp.bfloat16), "dp").astype(jnp.float32),
        lax.psum(gain_zero.astype(jnp.bfloat16), "dp").astype(jnp.float32),
        lax.psum(shift_zero.astype(jnp.bfloat16), "dp").astype(jnp.float32),
        lax.psum(gain_one.astype(jnp.bfloat16), "dp").astype(jnp.float32),
        lax.psum(shift_one.astype(jnp.bfloat16), "dp").astype(jnp.float32),
        lax.psum(dense_in_grad.astype(jnp.bfloat16), "dp").astype(jnp.float32),
        lax.psum(dense_out_grad.astype(jnp.bfloat16), "dp").astype(jnp.float32),
    )
    qkv_weight_grad = jnp.stack([qkv_lower, qkv_upper])
    out_weight_grad = jnp.stack([outw_lower, outw_upper])
    qv_bias_grad = jnp.stack([bias_lower, bias_upper])
    out_bias_grad = jnp.stack([outb_lower, outb_upper])
    ln_gain_grad = jnp.stack([gain_zero, gain_one, gain_two, gain_three])
    ln_bias_grad = jnp.stack([shift_zero, shift_one, shift_two, shift_three])
    return (
        output,
        input_grad,
        qkv_weight_grad,
        out_weight_grad,
        qv_bias_grad,
        out_bias_grad,
        ln_gain_grad,
        ln_bias_grad,
        dense_in_grad,
        dense_out_grad,
        router_grad,
        expert_in_grad,
        expert_out_grad,
    )


def solution(mesh):
    in_specs = (
        P("dp", None),
        P("dp", None),
        P("dp", None),
        P(None, None, None, "tensor"),
        P(None, "tensor", None),
        P(None, None, "tensor"),
        P(),
        P(),
        P(),
        P(None, "tensor"),
        P("tensor", None),
        P(),
        P("dp", None, "tensor"),
        P("dp", "tensor", None),
    )
    out_specs = (
        P("dp", None),
        P("dp", None),
        P(None, None, None, "tensor"),
        P(None, "tensor", None),
        P(None, None, "tensor"),
        P(),
        P(),
        P(),
        P(None, "tensor"),
        P("tensor", None),
        P(),
        P("dp", None, "tensor"),
        P("dp", "tensor", None),
    )
    return jax.shard_map(
        per_device, mesh=mesh, in_specs=in_specs, out_specs=out_specs, check_vma=False
    )
```

profile of v0, /device:TPU:0, one launch (start us, length us, event | category | flops | bytes accessed | tf_op | source)
XLA Modules:
  0.0 1160.7 jit_solution(18074685449843460773)
XLA Ops:
  18.9 45.3 %all-reduce.14.cloned.1.call-done = bf16[394,768]{1,0:T(8,128)(2,1)} async-done(((bf16[394,768]{1,0:T(8,128)(2,1)}), bf16[394,768]{1,0:T(8,128)(2,1)}) %all-reduce.14.cloned.1.call-update) | async-done | bytes 605200 | tf_op jit(solution)/shard_map/psum | solution.py:67
  76.1 39.0 %all-reduce.16.cloned.1.call-done = bf16[394,768]{1,0:T(8,128)(2,1)} async-done(((bf16[394,768]{1,0:T(8,128)(2,1)}), bf16[394,768]{1,0:T(8,128)(2,1)}) %all-reduce.16.cloned.1.call-update) | async-done | bytes 605200 | tf_op jit(solution)/shard_map/psum | solution.py:138
  127.3 40.2 %all-reduce.18.cloned.1.call-done = bf16[394,768]{1,0:T(8,128)(2,1)} async-done(((bf16[394,768]{1,0:T(8,128)(2,1)}), bf16[394,768]{1,0:T(8,128)(2,1)}) %all-reduce.18.cloned.1.call-update) | async-done | bytes 605200 | tf_op jit(solution)/shard_map/psum | solution.py:67
  175.9 7.4 all-to-all-start
  185.1 10.7 gather_fusion
  196.2 5.5 fusion.9
  204.4 6.1 all-to-all-done
  210.5 5.9 all-to-all-start.2
  219.2 12.0 %multiply_convert_fusion = (bf16[1184,768]{1,0:T(8,128)(2,1)}, f32[1184,768]{1,0:T(8,128)}, f32[1184,768]{1,0:T(8,128)}) fusion(bf16[1184,768]{1,0:T(8,128)(2,1)} %reshape.271, bf16[1,768,768]{2,1,0:T(8,128)(2,1)S(1)} %copy-done), kind=kOutput, calls=%fused_computation.10 | convolution fusion | flops 1455808512 | bytes 12091392 | tf_op jit(solution)/shard_map/dot_general | solution.py:179
  231.1 12.2 %all-to-all-done.2 = bf16[32,37,768]{2,1,0:T(8,128)(2,1)} async-done(((bf16[32,37,768]{2,1,0:T(8,128)(2,1)}), bf16[32,37,768]{2,1,0:T(8,128)(2,1)}, u32[]{:S(2)}, u32[]{:S(2)}) %all-to-all-start.2) | async-done | bytes 1818656 | tf_op jit(solution)/shard_map/all_to_all | solution.py:229
  246.0 7.3 add_convert_fusion
  260.6 5.5 all-to-all-start.3
  273.4 17.1 %all-to-all-done.3 = bf16[32,37,768]{2,1,0:T(8,128)(2,1)} async-done(((bf16[32,37,768]{2,1,0:T(8,128)(2,1)}), bf16[32,37,768]{2,1,0:T(8,128)(2,1)}, u32[]{:S(2)}, u32[]{:S(2)}) %all-to-all-start.3) | async-done | bytes 1818656 | tf_op jit(solution)/shard_map/all_to_all | solution.py:246
  299.7 6.8 gather_fusion.2
  310.5 5.7 select_reduce_fusion
  323.9 6.8 gather_fusion.1
  338.5 7.4 psum.201
  345.9 14.1 %all-reduce.20.cloned.1.call-done = bf16[394,768]{1,0:T(8,128)(2,1)} async-done(((bf16[394,768]{1,0:T(8,128)(2,1)}), bf16[394,768]{1,0:T(8,128)(2,1)}) %all-reduce.20.cloned.1.call-update) | async-done | bytes 605200 | tf_op jit(solution)/shard_map/psum | solution.py:257
  379.2 36.3 %all-reduce.22.cloned.1.call-done = bf16[394,768]{1,0:T(8,128)(2,1)} async-done(((bf16[394,768]{1,0:T(8,128)(2,1)}), bf16[394,768]{1,0:T(8,128)(2,1)}) %all-reduce.22.cloned.1.call-update) | async-done | bytes 605200 | tf_op jit(solution)/shard_map/psum | solution.py:122
  429.4 36.2 %all-reduce.24.cloned.1.call-done = bf16[394,768]{1,0:T(8,128)(2,1)} async-done(((bf16[394,768]{1,0:T(8,128)(2,1)}), bf16[394,768]{1,0:T(8,128)(2,1)}) %all-reduce.24.cloned.1.call-update) | async-done | bytes 605200 | tf_op jit(solution)/shard_map/psum | solution.py:150
  499.5 34.2 %all-reduce.30.cloned.1.call-done = (bf16[394,768]{1,0:T(8,128)(2,1)}, bf16[394,768]{1,0:T(8,128)(2,1)}) async-done(((bf16[394,768]{1,0:T(8,128)(2,1)}, bf16[394,768]{1,0:T(8,128)(2,1)}), (bf16[394,768]{1,0:T(8,128)(2,1)}, bf16[394,768]{1,0:T(8,128)(2,1)})) %all-reduce.30.cloned.1.call-update) | async-done | bytes 1210384 | tf_op jit(solution)/shard_map/psum | solution.py:194
  540.6 5.3 convolution_bitcast_fusion
  552.3 260.2 %all-reduce.26.cloned.1.call-done = (bf16[1,2,192]{2,1,0:T(2,128)(2,1)}, bf16[1,2,192]{2,1,0:T(2,128)(2,1)}, bf16[1,768]{1,0:T(2,128)(2,1)}, bf16[1,768]{1,0:T(2...) async-done(((bf16[1,2,192]{2,1,0:T(2,128)(2,1)}, ...) | async-done | bytes 66064 | tf_op jit(solution)/shard_map/psum | solution.py:342
  819.1 326.2 %all-reduce.28.cloned.1.call-done = (bf16[1,768,3,192]{1,3,2,0:T(8,128)(2,1)}, bf16[1,768,3,192]{1,3,2,0:T(8,128)(2,1)}, bf16[1,192,768]{2,1,0:T(8,128)(2,1)}, b...) async-done(((bf16[1,768,3,192]{1,3,2,0:T(8,128)(2,1)}, bf16[1,768,3,192]{1,3,2,0:T(8,128)(2,1)}, bf16[1,192,768]{2,1,0:T(8,128)(2,1)}, ...) | async-done | bytes 4718608 | tf_op jit(solution)/shard_map/psum | solution.py:340
  (441 shorter events, 191.6 us)
Async XLA Ops:
  7.2 212.0 %copy-start = (bf16[1,768,768]{2,1,0:T(8,128)(2,1)S(1)}, bf16[1,768,768]{2,1,0:T(8,128)(2,1)}, u32[]{:S(2)}) copy-start(bf16[1,768,768]{2,1,0:T(8,128)(2,1)} %param.28) | copy-start | bytes 3538948
  7.2 57.0 %all-reduce.14.cloned.1.call-start = ((), (), s32[]{:S(2)}) async-start(), calls=%async_computation.4 | async-start | bytes 1228800 | tf_op jit(solution)/shard_map/psum | solution.py:67
  12.7 53.5 %copy-start.68 = (f32[768]{0:T(1024)}, f32[768]{0:T(1024)S(1)}, u32[]{:S(2)}) copy-start(f32[768]{0:T(1024)S(1)} %get-tuple-element.107) | copy-start | bytes 9220
  12.7 53.5 %copy-start.101 = (f32[768]{0:T(1024)}, f32[768]{0:T(1024)S(1)}, u32[]{:S(2)}) copy-start(f32[768]{0:T(1024)S(1)} %get-tuple-element.34) | copy-start | bytes 9220
  12.7 104.2 %copy-start.62 = (f32[768]{0:T(1024)}, f32[768]{0:T(1024)S(1)}, u32[]{:S(2)}) copy-start(f32[768]{0:T(1024)S(1)} %get-tuple-element.105) | copy-start | bytes 9220
  12.7 104.2 %copy-start.103 = (f32[768]{0:T(1024)}, f32[768]{0:T(1024)S(1)}, u32[]{:S(2)}) copy-start(f32[768]{0:T(1024)S(1)} %get-tuple-element.36) | copy-start | bytes 9220
  12.7 156.8 %copy-start.64 = (f32[768]{0:T(1024)}, f32[768]{0:T(1024)S(1)}, u32[]{:S(2)}) copy-start(f32[768]{0:T(1024)S(1)} %get-tuple-element.108) | copy-start | bytes 9220
  17.6 48.1 %copy-start.37 = (bf16[394,192]{0,1:T(8,128)(2,1)}, bf16[394,192]{0,1:T(8,128)(2,1)S(1)}, u32[]{:S(2)}) copy-start(bf16[394,192]{0,1:T(8,128)(2,1)S(1)} %convert_element_type.295) | copy-start | bytes 453892
  18.8 96.2 %all-reduce.16.cloned.1.call-start = ((), (), s32[]{:S(2)}) async-start(), calls=%async_computation.5 | async-start | bytes 1228800 | tf_op jit(solution)/shard_map/psum | solution.py:138
  18.9 96.2 %copy-start.54 = (f32[768]{0:T(1024)}, f32[768]{0:T(1024)S(1)}, u32[]{:S(2)}) copy-start(f32[768]{0:T(1024)S(1)} %get-tuple-element.38) | copy-start | bytes 9220
  73.0 94.5 %all-reduce.18.cloned.1.call-start = ((), (), s32[]{:S(2)}) async-start(), calls=%async_computation.6 | async-start | bytes 1228800 | tf_op jit(solution)/shard_map/psum | solution.py:67
  73.3 48.1 %copy-start.90 = (f32[3,64]{1,0:T(4,128)}, f32[3,64]{1,0:T(4,128)S(1)}, u32[]{:S(2)}) copy-start(f32[3,64]{1,0:T(4,128)S(1)} %add.280) | copy-start | bytes 2308
  73.4 49.6 %copy-start.96 = (f32[3,64]{1,0:T(4,128)}, f32[3,64]{1,0:T(4,128)S(1)}, u32[]{:S(2)}) copy-start(f32[3,64]{1,0:T(4,128)S(1)} %add.277) | copy-start | bytes 2308
  175.9 34.6 %all-to-all-start = ((bf16[32,37,768]{2,1,0:T(8,128)(2,1)}), bf16[32,37,768]{2,1,0:T(8,128)(2,1)}, u32[]{:S(2)}, u32[]{:S(2)}) async-start(bf16[32,37,768]{2,1,0:T(8,128)(2,1)} %reshape.270), calls=%async_computation | async-start | bytes 3932160 | tf_op jit(solution)/shard_map/all_to_all | solution.py:175
  210.5 32.8 %all-to-all-start.2 = ((bf16[32,37,768]{2,1,0:T(8,128)(2,1)}), bf16[32,37,768]{2,1,0:T(8,128)(2,1)}, u32[]{:S(2)}, u32[]{:S(2)}) async-start(bf16[32,37,768]{2,1,0:T(8,128)(2,1)} %reshape.274), calls=%async_computation.2 | async-start | bytes 3932160 | tf_op jit(solution)/shard_map/all_to_all | solution.py:229
  260.6 29.8 %all-to-all-start.3 = ((bf16[32,37,768]{2,1,0:T(8,128)(2,1)}), bf16[32,37,768]{2,1,0:T(8,128)(2,1)}, u32[]{:S(2)}, u32[]{:S(2)}) async-start(bf16[32,37,768]{2,1,0:T(8,128)(2,1)} %convolution_convert_fusion.1), calls=%async_computation.3 | async-start | bytes 3932160 | tf_op jit(solution)/shard_map/all_to_all | solution.py:246
  290.5 30.2 %all-to-all-start.1 = ((bf16[32,37,768]{2,1,0:T(8,128)(2,1)}), bf16[32,37,768]{2,1,0:T(8,128)(2,1)}, u32[]{:S(2)}, u32[]{:S(2)}) async-start(bf16[32,37,768]{2,1,0:T(8,128)(2,1)} %convolution_convert_fusion.2), calls=%async_computation.1 | async-start | bytes 3932160 | tf_op jit(solution)/shard_map/all_to_all | solution.py:182
  295.7 64.4 %all-reduce.20.cloned.1.call-start = ((), (), s32[]{:S(2)}) async-start(), calls=%async_computation.7 | async-start | bytes 1228800 | tf_op jit(solution)/shard_map/psum | solution.py:257
  316.2 99.3 %all-reduce.22.cloned.1.call-start = ((), (), s32[]{:S(2)}) async-start(), calls=%async_computation.8 | async-start | bytes 1228800 | tf_op jit(solution)/shard_map/psum | solution.py:122
  373.5 92.1 %all-reduce.24.cloned.1.call-start = ((), (), s32[]{:S(2)}) async-start(), calls=%async_computation.9 | async-start | bytes 1228800 | tf_op jit(solution)/shard_map/psum | solution.py:150
  373.6 41.9 %copy-start.63 = (f32[768]{0:T(1024)S(1)}, f32[768]{0:T(1024)}, u32[]{:S(2)}) copy-start(f32[768]{0:T(1024)} %copy-done.62) | copy-start | bytes 9220
  423.5 110.1 %all-reduce.30.cloned.1.call-start = ((), (), s32[]{:S(2)}) async-start(), calls=%async_computation.12 | async-start | bytes 2457600 | tf_op jit(solution)/shard_map/psum | solution.py:194
  487.4 325.1 %all-reduce.26.cloned.1.call-start = ((), (), s32[]{:S(2)}) async-start(), calls=%async_computation.10 | async-start | bytes 163840 | tf_op jit(solution)/shard_map/psum | solution.py:342
  537.9 607.4 %all-reduce.28.cloned.1.call-start = ((), (), s32[]{:S(2)}) async-start(), calls=%async_computation.11 | async-start | bytes 9437184 | tf_op jit(solution)/shard_map/psum | solution.py:340
  (105 other events, 673.7 us)
Sparse Core Ops, SparseCore 0:
  19.0 45.1 all-reduce.13
  73.1 41.9 all-reduce.15
  125.6 41.8 all-reduce.17
  316.3 43.6 all-reduce.19
  373.6 41.8 all-reduce.21
  423.6 41.8 all-reduce.23
  487.5 46.0 all-reduce.29
  538.9 273.5 all-reduce.25
  816.6 328.6 all-reduce.27
where the time goes:
time: 1170 us; the launch traced here: 1160 us
  waiting for transfers between devices  871 us (74%)
  local copies, waits for them, and re-layouts  92.8 us (8%)
  matrix products  89.6 us (8%)
  other arithmetic  58.1 us (5%)
  starting transfers between devices  25.3 us (2%)
  between operations  16 us (1%)
    psum x1, waiting for transfers between devices, per_device(): lax.psum(qkv_upper.astype(jnp.bfloat16), 'dp').astype(jnp.float32)  326 us
    psum x1, waiting for transfers between devices, per_device(): lax.psum(bias_upper.astype(jnp.bfloat16), 'dp').astype(jnp.float32)  260 us
    psum x2, waiting for transfers between devices, attend_forward(): lax.psum(partial_out.astype(jnp.bfloat16), 'tensor').astype(jnp.float32)  85.4 us
    psum x1, waiting for transfers between devices, dense_forward(): lax.psum(partial_out.astype(jnp.bfloat16), 'tensor').astype(jnp.float32)  39 us
    psum x1, waiting for transfers between devices, attend_backward(): lax.psum(normed_part.astype(jnp.bfloat16), 'tensor').astype(jnp.float32)  36.3 us
    psum x1, waiting for transfers between devices, dense_backward(): lax.psum(normed_part.astype(jnp.bfloat16), 'tensor').astype(jnp.float32)  36.2 us
    psum x1, waiting for transfers between devices, moe_forward(): lax.psum(mixed_part.astype(jnp.bfloat16), 'tensor').astype(jnp.float32)  34.2 us
  transfers between devices with their start and end apart: 13, of which 13 were waited for; matrix products, arithmetic and copies ran while one was open for 11% of the time, Pallas kernels for 0%

commit v1 on v0

--- a/solution.py
+++ b/solution.py
@@ -1,6 +1,10 @@
+import functools
+
 import jax
 import jax.numpy as jnp
 from jax import lax
+from jax.experimental import pallas as pl
+from jax.experimental.pallas import tpu as pltpu
 from jax.sharding import PartitionSpec as P
 
 HEAD = 64
@@ -10,6 +14,328 @@
 epsilon = 1e-06
 bfloat = jnp.bfloat16
 single = jnp.float32
+
+
+MESH = pl.DeviceIdType.MESH
+
+
+def tensor_sum_kernel(count, rows, p_ref, o_ref, got_one, sum_one, got_two, sum_two, got_three, sems):
+    t = lax.axis_index("tensor")
+    core = lax.rem(t, 2)
+    sibling = {"tensor": t + 1 - 2 * core}
+    opposite = {"tensor": lax.rem(t + 2, 4)}
+    barrier = pltpu.get_barrier_semaphore()
+    for peer in (sibling, opposite):
+        pl.semaphore_signal(barrier, inc=1, device_id=peer, device_id_type=MESH)
+    pl.semaphore_wait(barrier, 2)
+
+    def columns(which, j):
+        return pl.ds(pl.multiple_of((which * count + j) * 128, 128), 128)
+
+    def copy(source, target, step, j, peer):
+        return pltpu.make_async_remote_copy(
+            src_ref=source,
+            dst_ref=target,
+            send_sem=sems.at[0, step, j],
+            recv_sem=sems.at[1, step, j],
+            device_id=peer,
+            device_id_type=MESH,
+        )
+
+    first = [copy(p_ref.at[:, columns(1 - core, j)], got_one.at[j], 0, j, sibling) for j in range(count)]
+    second = [copy(sum_one.at[j], got_two.at[j], 1, j, opposite) for j in range(count)]
+    third = [copy(sum_two.at[j], got_three.at[j], 2, j, sibling) for j in range(count)]
+    for j in range(count):
+        first[j].start()
+    for j in range(count):
+        first[j].wait_recv()
+        own = p_ref[:, columns(core, j)].astype(single)
+        sum_one[j] = (own + got_one[j].astype(single)).astype(bfloat)
+        second[j].start()
+    for j in range(count):
+        second[j].wait_recv()
+        whole = (sum_one[j].astype(single) + got_two[j].astype(single)).astype(bfloat)
+        sum_two[j] = whole
+        third[j].start()
+        o_ref[:, columns(core, j)] = whole
+    for j in range(count):
+        third[j].wait_recv()
+        o_ref[:, columns(1 - core, j)] = got_three[j]
+    for j in range(count):
+        first[j].wait_send()
+        second[j].wait_send()
+        third[j].wait_send()
+
+
+def tensor_sum(partial, collective_id):
+    rows, width = partial.shape
+    count = width // 256
+    block = pltpu.VMEM((count, rows, 128), bfloat)
+    return pl.pallas_call(
+        functools.partial(tensor_sum_kernel, count, rows),
+        out_shape=jax.ShapeDtypeStruct((rows, width), bfloat),
+        in_specs=[pl.BlockSpec(memory_space=pltpu.VMEM)],
+        out_specs=pl.BlockSpec(memory_space=pltpu.VMEM),
+        scratch_shapes=[block] * 5 + [pltpu.SemaphoreType.DMA((2, 3, count))],
+        compiler_params=pltpu.CompilerParams(
+            collective_id=collective_id, has_side_effects=True, vmem_limit_bytes=32 * 2**20
+        ),
+        name="tensor_sum",
+    )(partial)
+
+
+BIG = 3072
+HALF = BIG // 2
+PART = HALF // 4
+PIECE = PART // 4
+SMALL = 48
+
+
+def add_rows(target, target_row, sources, rows):
+    def body(i, carry):
+        total = None
+        for ref, row in sources:
+            value = ref[pl.ds(pl.multiple_of(row + i * 16, 16), 16), :].astype(single)
+            total = value if total is None else total + value
+        target[pl.ds(pl.multiple_of(target_row + i * 16, 16), 16), :] = total.astype(bfloat)
+        return carry
+
+    lax.fori_loop(0, rows // 16, body, 0)
+
+
+def grad_sum_kernel(*refs):
+    ins, small_in = refs[:6], refs[6]
+    outs, small_out = refs[7:13], refs[13]
+    (given, result, near_a, near_b, left_a, right_a, left_b, right_b, pass_a, pass_b, sum_a, sum_b) = refs[14:26]
+    (near_c, near_d, left_c, right_c, left_d, right_d, pass_c, pass_d, sum_c, sum_d) = refs[26:36]
+    z_got, small_x, small_y, small_z, small_one, small_two = refs[36:42]
+    local_sem, send_sem, recv_sem, small_send, small_recv = refs[42:47]
+
+    dp = lax.axis_index("dp")
+    plane, x, y = dp // 16, lax.rem(dp // 4, 4), lax.rem(dp, 4)
+
+    def at(plane_to, x_to, y_to):
+        return {"dp": plane_to * 16 + x_to * 4 + y_to}
+
+    def along_x(step):
+        return at(plane, lax.rem(x + step, 4), y)
+
+    def along_y(step):
+        return at(plane, x, lax.rem(y + step, 4))
+
+    across = at(1 - plane, x, y)
+    barrier = pltpu.get_barrier_semaphore()
+    peers = [along_x(1), along_x(2), along_x(3), along_y(1), along_y(2), along_y(3), across]
+    for peer in peers:
+        pl.semaphore_signal(barrier, inc=1, device_id=peer, device_id_type=MESH)
+
+    sizes = [ref.shape[0] for ref in ins]
+    starts = [sum(sizes[:i]) for i in range(6)]
+    loads = [
+        pltpu.make_async_copy(ins[i], given.at[pl.ds(starts[i], sizes[i]), :], local_sem.at[i])
+        for i in range(6)
+    ]
+    for load in loads:
+        load.start()
+    for load in loads:
+        load.wait()
+    pl.semaphore_wait(barrier, 7)
+
+    used = []
+
+    def send(source, target, peer):
+        k = len(used)
+        copy = pltpu.make_async_remote_copy(
+            src_ref=source,
+            dst_ref=target,
+            send_sem=send_sem.at[k],
+            recv_sem=recv_sem.at[k],
+            device_id=peer,
+            device_id_type=MESH,
+        )
+        used.append(copy)
+        copy.start()
+        return copy
+
+    small_used = []
+
+    def send_small(source, target, peer):
+        k = len(small_used)
+        copy = pltpu.make_async_remote_copy(
+            src_ref=source,
+            dst_ref=target,
+            send_sem=small_send.at[k],
+            recv_sem=small_recv.at[k],
+            device_id=peer,
+            device_id_type=MESH,
+        )
+        small_used.append(copy)
+        copy.start()
+        return copy
+
+    def rows_of(ref, row, count):
+        return ref.at[pl.ds(pl.multiple_of(row, 16), count), :]
+
+    class Scatter:
+        def __init__(self, source, base, size, place, along, near, left, right, onward, total):
+            self.source, self.base, self.size, self.place = source, base, size, place
+            self.along, self.near, self.left, self.right = along, near, left, right
+            self.onward, self.total = onward, total
+
+        def row(self, step):
+            return self.base + lax.rem(self.place + step, 4) * self.size
+
+        def start(self):
+            half = self.size // 2
+            s = self.source
+            self.far_right = send(rows_of(s, self.row(2), half), rows_of(self.near, 0, half), self.along(1))
+            self.far_left = send(rows_of(s, self.row(2) + half, half), rows_of(self.near, half, half), self.along(3))
+            self.to_right = send(rows_of(s, self.row(1) + half, half), rows_of(self.left, half, half), self.along(1))
+            self.to_left = send(rows_of(s, self.row(3), half), rows_of(self.right, 0, half), self.along(3))
+
+        def middle(self):
+            half = self.size // 2
+            s = self.source
+            self.far_right.wait_recv()
+            add_rows(self.onward, 0, [(s, self.row(1)), (self.near, 0)], half)
+            self.on_right = send(rows_of(self.onward, 0, half), rows_of(self.left, 0, half), self.along(1))
+            self.far_left.wait_recv()
+            add_rows(self.onward, half, [(s, self.row(3) + half), (self.near, half)], half)
+            self.on_left = send(rows_of(self.onward, half, half), rows_of(self.right, half, half), self.along(3))
+
+        def finish(self):
+            for copy in (self.to_right, self.to_left, self.on_right, self.on_left):
+                copy.wait_recv()
+            add_rows(self.total, 0, [(self.source, self.row(0)), (self.left, 0), (self.right, 0)], self.size)
+
+    class Gather:
+        def __init__(self, base, size, place, along):
+            self.base, self.size, self.place, self.along = base, size, place, along
+
+        def row(self, step):
+            return self.base + lax.rem(self.place + step, 4) * self.size
+
+        def start(self):
+            own, half = self.row(0), self.size // 2
+            first, second = rows_of(result, own, half), rows_of(result, own + half, half)
+            self.right_one = send(first, first, self.along(1))
+            self.left_two = send(second, second, self.along(3))
+            self.right_two = send(second, second, self.along(1))
+            self.left_one = send(first, first, self.along(3))
+
+        def middle(self):
+            half = self.size // 2
+            self.right_one.wait_recv()
+            from_left = rows_of(result, self.row(3), half)
+            self.on_right = send(from_left, from_left, self.along(1))
+            self.left_two.wait_recv()
+            from_right = rows_of(result, self.row(1) + half, half)
+            self.on_left = send(from_right, from_right, self.along(3))
+
+        def finish(self):
+            for copy in (self.right_two, self.left_one, self.on_right, self.on_left):
+                copy.wait_recv()
+
+    def together(parts):
+        for part in parts:
+            part.start()
+        for part in parts:
+            part.middle()
+        for part in parts:
+            part.finish()
+
+    def add_small(target, ref, count):
+        def body(i, carry):
+            at_rows = pl.ds(pl.multiple_of(i * 16, 16), 16)
+            total = ref[0, at_rows, :].astype(single)
+            for k in range(1, count):
+                total = total + ref[k, at_rows, :].astype(single)
+            target[at_rows, :] = total.astype(bfloat)
+            return carry
+
+        lax.fori_loop(0, SMALL // 16, body, 0)
+
+    small_x[x] = small_in[...]
+    first_small = [send_small(small_in, small_x.at[x], along_x(k)) for k in (1, 2, 3)]
+    together(
+        [
+            Scatter(given, 0, PART, x, along_x, near_a, left_a, right_a, pass_a, sum_a),
+            Scatter(given, HALF, PART, y, along_y, near_b, left_b, right_b, pass_b, sum_b),
+        ]
+    )
+    for copy in first_small:
+        copy.wait_recv()
+    add_small(small_one, small_x, 4)
+    small_y[y] = small_one[...]
+    second_small = [send_small(small_one, small_y.at[y], along_y(k)) for k in (1, 2, 3)]
+    together(
+        [
+            Scatter(sum_a, 0, PIECE, y, along_y, near_c, left_c, right_c, pass_c, sum_c),
+            Scatter(sum_b, 0, PIECE, x, along_x, near_d, left_d, right_d, pass_d, sum_d),
+        ]
+    )
+    for copy in second_small:
+        copy.wait_recv()
+    add_small(small_two, small_y, 4)
+    small_z[plane] = small_two[...]
+    pair_small = send_small(small_two, small_z.at[plane], across)
+    pair_a = send(sum_c, rows_of(z_got, 0, PIECE), across)
+    pair_b = send(sum_d, rows_of(z_got, PIECE, PIECE), across)
+    row_a = x * PART + y * PIECE
+    row_b = HALF + y * PART + x * PIECE
+    pair_a.wait_recv()
+    add_rows(result, row_a, [(sum_c, 0), (z_got, 0)], PIECE)
+    pair_b.wait_recv()
+    add_rows(result, row_b, [(sum_d, 0), (z_got, PIECE)], PIECE)
+    together([Gather(x * PART, PIECE, y, along_y), Gather(HALF + y * PART, PIECE, x, along_x)])
+    together([Gather(0, PART, x, along_x), Gather(HALF, PART, y, along_y)])
+    stores = [
+        pltpu.make_async_copy(result.at[pl.ds(starts[i], sizes[i]), :], outs[i], local_sem.at[i])
+        for i in range(6)
+    ]
+    for store in stores:
+        store.start()
+    pair_small.wait_recv()
+    add_small(small_out, small_z, 2)
+    for copy in used:
+        copy.wait_send()
+    for copy in small_used:
+        copy.wait_send()
+    for store in stores:
+        store.wait()
+
+
+def grad_sum(arrays, small, collective_id):
+    def rows(count):
+        return pltpu.VMEM((count, 768), bfloat)
+
+    scratch = [rows(BIG), rows(BIG)]
+    scratch += [rows(PART)] * 10
+    scratch += [rows(PIECE)] * 10
+    scratch += [rows(2 * PIECE)]
+    scratch += [pltpu.VMEM((4, SMALL, 768), bfloat)] * 2 + [pltpu.VMEM((2, SMALL, 768), bfloat)]
+    scratch += [rows(SMALL)] * 2
+    scratch += [
+        pltpu.SemaphoreType.DMA((6,)),
+        pltpu.SemaphoreType.DMA((50,)),
+        pltpu.SemaphoreType.DMA((50,)),
+        pltpu.SemaphoreType.DMA((7,)),
+        pltpu.SemaphoreType.DMA((7,)),
+    ]
+    hbm = pl.BlockSpec(memory_space=pl.ANY)
+    vmem = pl.BlockSpec(memory_space=pltpu.VMEM)
+    return pl.pallas_call(
+        grad_sum_kernel,
+        out_shape=[jax.ShapeDtypeStruct(a.shape, bfloat) for a in arrays]
+        + [jax.ShapeDtypeStruct(small.shape, bfloat)],
+        in_specs=[hbm] * 6 + [vmem],
+        out_specs=[hbm] * 6 + [vmem],
+        scratch_shapes=scratch,
+        compiler_params=pltpu.CompilerParams(
+            collective_id=collective_id, has_side_effects=True, vmem_limit_bytes=40 * 2**20
+        ),
+        name="grad_sum",
+    )(*arrays, small)
 
 
 def norm_forward(inputs, gain_row, shift_row):
@@ -64,7 +390,7 @@
     context = jnp.einsum("bhqk,bkhd->bqhd", probs_low, value_rows, preferred_element_type=single)
     context = context.reshape(tokens_here, local_width).astype(bfloat)
     partial_out = jnp.dot(context, out_weight[layer_index], preferred_element_type=single)
-    summed = lax.psum(partial_out.astype(jnp.bfloat16), "tensor").astype(jnp.float32)
+    summed = tensor_sum(partial_out.astype(jnp.bfloat16), 1).astype(jnp.float32)
     stored = (normal, inverse, normed_low, queries, key_rows, value_rows, log_total, context)
     return (inputs + summed + out_bias[layer_index], stored)
 
@@ -119,7 +445,7 @@
     normed_part = jnp.einsum(
         "tcf,dcf->td", stacked, qkv_weight[layer_index], preferred_element_type=single
     )
-    grad_normed = lax.psum(normed_part.astype(jnp.bfloat16), "tensor").astype(jnp.float32)
+    grad_normed = tensor_sum(normed_part.astype(jnp.bfloat16), 1).astype(jnp.float32)
     grad_in, gain_part, shift_part = norm_backward(
         grad_normed, normal, inverse, ln_gain[2 * layer_index]
     )
@@ -135,7 +461,7 @@
     pre_act = jnp.dot(normed_low, dense_in, preferred_element_type=single)
     activated = gelu_exact(pre_act).astype(bfloat)
     partial_out = jnp.dot(activated, dense_out, preferred_element_type=single)
-    summed = lax.psum(partial_out.astype(jnp.bfloat16), "tensor").astype(jnp.float32)
+    summed = tensor_sum(partial_out.astype(jnp.bfloat16), 1).astype(jnp.float32)
     return (inputs + summed, (normal, inverse, normed_low, pre_act, activated))
 
 
@@ -147,7 +473,7 @@
     grad_pre = gelu_slope(pre_act, grad_act).astype(bfloat)
     in_part = jnp.einsum("td,tf->df", normed_low, grad_pre, preferred_element_type=single)
     normed_part = jnp.einsum("tf,df->td", grad_pre, dense_in, preferred_element_type=single)
-    grad_normed = lax.psum(normed_part.astype(jnp.bfloat16), "tensor").astype(jnp.float32)
+    grad_normed = tensor_sum(normed_part.astype(jnp.bfloat16), 1).astype(jnp.float32)
     grad_in, gain_part, shift_part = norm_backward(grad_normed, normal, inverse, ln_gain[1])
     return (grad_out + grad_in, (in_part, out_part, gain_part, shift_part))
 
@@ -191,7 +517,7 @@
     activated = act_rows.reshape(sources, items, hidden_width)
     picked = jnp.take(back_rows.reshape(expert_count * capacity, feature_width), slot_index, axis=0)
     mixed_part = jnp.sum(gate_values[:, :, None] * picked, axis=1)
-    mixed = lax.psum(mixed_part.astype(jnp.bfloat16), "tensor").astype(jnp.float32)
+    mixed = tensor_sum(mixed_part.astype(jnp.bfloat16), 1).astype(jnp.float32)
     stored = (
         normal,
         inverse,
@@ -254,7 +580,7 @@
         jnp.take(returned.reshape(row_count, feature_width), slot_index, axis=0), axis=1
     )
     grad_experts, grad_gates = (
-        lax.psum(normed_part.astype(jnp.bfloat16), "tensor").astype(jnp.float32),
+        tensor_sum(normed_part.astype(jnp.bfloat16), 1).astype(jnp.float32),
         lax.psum(gate_part.astype(jnp.bfloat16), "tensor").astype(jnp.float32),
     )
     grad_chosen = gate_values * (
@@ -316,53 +642,36 @@
         grad_one, 0, stored_one, qkv_weight, out_weight, ln_gain
     )
     qkv_lower, outw_lower, bias_lower, outb_lower, gain_zero, shift_zero = lower_parts
-    (
-        qkv_upper,
+    local_width = qkv_lower.shape[2]
+    arrays = [
+        jnp.transpose(qkv_lower, (1, 2, 0)).reshape(3 * local_width, -1),
+        jnp.transpose(qkv_upper, (1, 2, 0)).reshape(3 * local_width, -1),
+        outw_lower,
         outw_upper,
-        bias_upper,
-        outb_upper,
-        gain_two,
-        shift_two,
-        router_grad,
-        gain_three,
-        shift_three,
-        qkv_lower,
-        outw_lower,
-        bias_lower,
-        outb_lower,
-        gain_zero,
-        shift_zero,
-        gain_one,
-        shift_one,
         dense_in_grad,
         dense_out_grad,
-    ) = (
-        lax.psum(qkv_upper.astype(jnp.bfloat16), "dp").astype(jnp.float32),
-        lax.psum(outw_upper.astype(jnp.bfloat16), "dp").astype(jnp.float32),
-        lax.psum(bias_upper.astype(jnp.bfloat16), "dp").astype(jnp.float32),
-        lax.psum(outb_upper.astype(jnp.bfloat16), "dp").astype(jnp.float32),
-        lax.psum(gain_two.astype(jnp.bfloat16), "dp").astype(jnp.float32),
-        lax.psum(shift_two.astype(jnp.bfloat16), "dp").astype(jnp.float32),
-        lax.psum(router_grad.astype(jnp.bfloat16), "dp").astype(jnp.float32),
-        lax.psum(gain_three.astype(jnp.bfloat16), "dp").astype(jnp.float32),
-        lax.psum(shift_three.astype(jnp.bfloat16), "dp").astype(jnp.float32),
-        lax.psum(qkv_lower.astype(jnp.bfloat16), "dp").astype(jnp.float32),
-        lax.psum(outw_lower.astype(jnp.bfloat16), "dp").astype(jnp.float32),
-        lax.psum(bias_lower.astype(jnp.bfloat16), "dp").astype(jnp.float32),
-        lax.psum(outb_lower.astype(jnp.bfloat16), "dp").astype(jnp.float32),
-        lax.psum(gain_zero.astype(jnp.bfloat16), "dp").astype(jnp.float32),
-        lax.psum(shift_zero.astype(jnp.bfloat16), "dp").astype(jnp.float32),
-        lax.psum(gain_one.astype(jnp.bfloat16), "dp").astype(jnp.float32),
-        lax.psum(shift_one.astype(jnp.bfloat16), "dp").astype(jnp.float32),
-        lax.psum(dense_in_grad.astype(jnp.bfloat16), "dp").astype(jnp.float32),
-        lax.psum(dense_out_grad.astype(jnp.bfloat16), "dp").astype(jnp.float32),
-    )
-    qkv_weight_grad = jnp.stack([qkv_lower, qkv_upper])
-    out_weight_grad = jnp.stack([outw_lower, outw_upper])
-    qv_bias_grad = jnp.stack([bias_lower, bias_upper])
-    out_bias_grad = jnp.stack([outb_lower, outb_upper])
-    ln_gain_grad = jnp.stack([gain_zero, gain_one, gain_two, gain_three])
-    ln_bias_grad = jnp.stack([shift_zero, shift_one, shift_two, shift_three])
+    ]
+    small = jnp.concatenate(
+        [
+            router_grad.T,
+            jnp.stack([gain_zero, gain_one, gain_two, gain_three]),
+            jnp.stack([shift_zero, shift_one, shift_two, shift_three]),
+            jnp.stack([outb_lower, outb_upper]),
+            jnp.stack([bias_lower, bias_upper]).reshape(1, -1),
+            jnp.zeros((5, router_grad.shape[0]), single),
+        ]
+    )
+    summed = grad_sum([a.astype(bfloat) for a in arrays], small.astype(bfloat), 2)
+    big = [a.astype(single) for a in summed]
+    small = big[6]
+    qkv_weight_grad = jnp.transpose(
+        jnp.stack([big[0], big[1]]).reshape(2, 3, local_width, -1), (0, 3, 1, 2)
+    )
+    out_weight_grad = jnp.stack([big[2], big[3]])
+    dense_in_grad, dense_out_grad = big[4], big[5]
+    router_grad = small[:32].T
+    ln_gain_grad, ln_bias_grad, out_bias_grad = small[32:36], small[36:40], small[40:42]
+    qv_bias_grad = small[42].reshape(2, 2, local_width)
     return (
         output,
         input_grad,

time: 1170 us -> 466 us (0.40)
  waiting for transfers between devices: 871 us -> 34.9 us
  Pallas kernels: 0 us -> 186 us
  other arithmetic: 58.1 us -> 31.6 us
  matrix products: 89.6 us -> 74.6 us
  between operations: 16 us -> 3.22 us
    psum x9 -> x0, waiting for transfers between devices: 832 us -> none  [the longest x1 326 us: per_device(): lax.psum(qkv_upper.astype(jnp.bfloat16), 'dp').astype(jnp.float32)]
    pallas_call x0 -> x9, Pallas kernels: none -> 186 us  [the longest x8 108 us: tensor_sum(): pl.pallas_call(functools.partial(tensor_sum_kernel, count, rows), out_sha...]
    unnamed x237 -> x275, local copies, waits for them, and re-layouts: 13.2 us -> 26.5 us
  transfers between devices with their start and end apart: 13 -> 4, of which waited for: 13 -> 3; matrix products, arithmetic and copies ran while one was open for 11% -> 15% of each run, Pallas kernels for 0% -> 3%
where the time goes in v1:
time: 466 us; the launch traced here: 460 us
  Pallas kernels  186 us (40%)
  local copies, waits for them, and re-layouts  95.2 us (20%)
  matrix products  74.6 us (16%)
  waiting for transfers between devices  34.9 us (7%)
  other arithmetic  31.6 us (7%)
  starting transfers between devices  25.5 us (5%)
  blocking collectives  9.23 us (2%)
    pallas_call x8, Pallas kernels, tensor_sum(): pl.pallas_call(functools.partial(tensor_sum_kernel, count, rows), out_sha...  108 us
    pallas_call x1, Pallas kernels, grad_sum(): pl.pallas_call(grad_sum_kernel, out_shape=[jax.ShapeDtypeStruct(a.shape,...  77.7 us
    unnamed x275, local copies, waits for them, and re-layouts  26.5 us
    all_to_all x1, waiting for transfers between devices, moe_backward(): lax.all_to_all(rows_back.reshape(expert_count, capacity, feature_width).a...  16.3 us
    all_to_all x1, waiting for transfers between devices, moe_backward(): lax.all_to_all(outgoing.reshape(expert_count, capacity, feature_width), '...  13.1 us
    dot_general x1, matrix products, moe_forward(): pre_rows = jnp.dot(rows_flat, expert_in[0], preferred_element_type=single)  12 us
    gather x5, local copies, waits for them, and re-layouts, moe_forward(): chosen = jnp.take_along_axis(logits, routes, axis=1)  11.2 us
    gather x2, local copies, waits for them, and re-layouts, moe_backward(): jnp.take(returned.reshape(row_count, feature_width), slot_index, axis=0)  10.8 us
  transfers between devices with their start and end apart: 4, of which 3 were waited for; matrix products, arithmetic and copies ran while one was open for 15% of the time, Pallas kernels for 3%

profile of v1, /device:TPU:0, one launch (start us, length us, event | category | flops | bytes accessed | tf_op | source)
XLA Modules:
  0.0 459.8 jit_solution(15471945869033359032)
XLA Ops:
  10.8 14.0 %tensor_sum.8 = bf16[394,768]{1,0:T(8,128)(2,1)S(1)} custom-call(bf16[394,768]{1,0:T(8,128)(2,1)S(1)} %convolution_convert_fusion.10.p_ref), custom_call_target="tpu_custom_call" | custom-call | tf_op jit(solution)/shard_map/tensor_sum/pallas_call | solution.py:74
  32.5 13.6 %tensor_sum.9 = bf16[394,768]{1,0:T(8,128)(2,1)S(1)} custom-call(bf16[394,768]{1,0:T(8,128)(2,1)S(1)} %convolution_convert_fusion.9.p_ref), custom_call_target="tpu_custom_call" | custom-call | tf_op jit(solution)/shard_map/tensor_sum/pallas_call | solution.py:74
  56.7 13.5 %tensor_sum.10 = bf16[394,768]{1,0:T(8,128)(2,1)S(1)} custom-call(bf16[394,768]{1,0:T(8,128)(2,1)S(1)} %convolution_convert_fusion.8.p_ref), custom_call_target="tpu_custom_call" | custom-call | tf_op jit(solution)/shard_map/tensor_sum/pallas_call | solution.py:74
  79.3 8.9 %all-to-all-start = ((bf16[32,37,768]{2,1,0:T(8,128)(2,1)}), bf16[32,37,768]{2,1,0:T(8,128)(2,1)S(1)}, u32[]{:S(2)}, u32[]{:S(2)}) async-start(bf16[32,37,768]{2,1,0:T(8,128)(2,1)} %reshape.285), calls=%async_computation | async-start | bytes 3932160 | tf_op jit(solution)/shard_map/all_to_all | solution.py:501
  90.0 10.7 %gather_fusion = f32[788]{0:T(1024)S(1)} fusion(f32[394,32]{0,1:T(8,128)S(1)} %fusion.160, s32[788]{0:T(1024)S(1)} %reshape.325), kind=kCustom, calls=%fused_computation.2 | custom fusion | bytes 12608 | tf_op jit(solution)/shard_map/jit(take_along_axis)/gather | solution.py:485
  110.1 5.4 %all-to-all-done = bf16[32,37,768]{2,1,0:T(8,128)(2,1)S(1)} async-done(((bf16[32,37,768]{2,1,0:T(8,128)(2,1)}), bf16[32,37,768]{2,1,0:T(8,128)(2,1)S(1)}, u32[]{:S(2)}, u32[]{:S(2)}) %all-to-all-start) | async-done | bytes 1818656 | tf_op jit(solution)/shard_map/all_to_all | solution.py:501
  115.5 5.4 %all-to-all-start.2 = ((bf16[32,37,768]{2,1,0:T(8,128)(2,1)}), bf16[32,37,768]{2,1,0:T(8,128)(2,1)}, u32[]{:S(2)}, u32[]{:S(2)}) async-start(bf16[32,37,768]{2,1,0:T(8,128)(2,1)} %reshape.289), calls=%async_computation.2 | async-start | bytes 3932160 | tf_op jit(solution)/shard_map/all_to_all | solution.py:555
  122.5 12.0 %multiply_convert_fusion = (bf16[1184,768]{1,0:T(8,128)(2,1)}, f32[1184,768]{1,0:T(8,128)}, f32[1184,768]{1,0:T(8,128)}) fusion(bf16[1184,768]{1,0:T(8,128)(2,1)} %reshape.286, bf16[1,768,768]{2,1,0:T(8,128)(2,1)S(1)} %copy-done), kind=kOutput, calls=%fused_computation.10 | convolution fusion | flops 1455808512 | bytes 12091392 | tf_op jit(solution)/shard_map/dot_general | solution.py:505
  134.5 13.1 %all-to-all-done.2 = bf16[32,37,768]{2,1,0:T(8,128)(2,1)} async-done(((bf16[32,37,768]{2,1,0:T(8,128)(2,1)}), bf16[32,37,768]{2,1,0:T(8,128)(2,1)}, u32[]{:S(2)}, u32[]{:S(2)}) %all-to-all-start.2) | async-done | bytes 1818656 | tf_op jit(solution)/shard_map/all_to_all | solution.py:555
  150.7 7.2 %add_convert_fusion = bf16[1184,768]{1,0:T(8,128)(2,1)} fusion(f32[1184,768]{1,0:T(8,128)} %get-tuple-element.66, f32[1184,768]{1,0:T(8,128)} %get-tuple-element.87, bf16[1184,768]{1,0:T(8,128)(2,1)S(1)} %reshape.290, bf16[1,768,768]{2,1,0:T(8,128)(2,1)} %param.29), kind=kOutput, calls=%fused_computation.9 | convolution fusion | flops 1409433600 | bytes 12091392 | tf_op jit(solution)/shard_map/sd,fd->sf/dot_general | solution.py:568
  162.6 5.8 %all-to-all-start.3 = ((bf16[32,37,768]{2,1,0:T(8,128)(2,1)}), bf16[32,37,768]{2,1,0:T(8,128)(2,1)S(1)}, u32[]{:S(2)}, u32[]{:S(2)}) async-start(bf16[32,37,768]{2,1,0:T(8,128)(2,1)} %convolution_convert_fusion.1), calls=%async_computation.3 | async-start | bytes 3932160 | tf_op jit(solution)/shard_map/all_to_all | solution.py:572
  176.3 16.3 %all-to-all-done.3 = bf16[32,37,768]{2,1,0:T(8,128)(2,1)S(1)} async-done(((bf16[32,37,768]{2,1,0:T(8,128)(2,1)}), bf16[32,37,768]{2,1,0:T(8,128)(2,1)S(1)}, u32[]{:S(2)}, u32[]{:S(2)}) %all-to-all-start.3) | async-done | bytes 1818656 | tf_op jit(solution)/shard_map/all_to_all | solution.py:572
  192.7 5.4 %all-to-all-start.1 = ((bf16[32,37,768]{2,1,0:T(8,128)(2,1)}), bf16[32,37,768]{2,1,0:T(8,128)(2,1)}, u32[]{:S(2)}, u32[]{:S(2)}) async-start(bf16[32,37,768]{2,1,0:T(8,128)(2,1)} %convolution_convert_fusion.2), calls=%async_computation.1 | async-start | bytes 3932160 | tf_op jit(solution)/shard_map/all_to_all | solution.py:508
  198.4 5.3 %convolution_bitcast_fusion = f32[1,768,768]{2,1,0:T(8,128)} fusion(bf16[1184,768]{1,0:T(8,128)(2,1)} %get-tuple-element.65, bf16[1184,768]{1,0:T(8,128)(2,1)} %copy-done.51), kind=kOutput, calls=%fused_computation.40 | convolution fusion | flops 1396703232 | bytes 5996544 | tf_op jit(solution)/shard_map/sf,sd->fd/dot_general | solution.py:567
  208.9 6.8 %gather_fusion.2 = f32[788,768]{1,0:T(8,128)} fusion(f32[1184,768]{1,0:T(8,128)} %reshape.304, s32[1024]{0:T(1024)S(1)} %pad_clamp_fusion), kind=kCustom, calls=%fused_computation.1.clone | custom fusion | bytes 4844624 | tf_op jit(solution)/shard_map/jit(_take)/gather | solution.py:580
  219.7 4.9 %select_reduce_fusion.p_ref = bf16[394,768]{1,0:T(8,128)(2,1)S(1)} fusion(f32[394,2,768]{2,1,0:T(2,128)} %reshape.347, pred[394,2]{1,0:T(8,128)(4,1)S(1)} %copy.190), kind=kLoop, calls=%fused_computation.31 | loop fusion | flops 907776 | bytes 3026708 | tf_op jit(solution)/shard_map/reduce_sum | solution.py:579
  224.6 13.5 %tensor_sum.12 = bf16[394,768]{1,0:T(8,128)(2,1)S(1)} custom-call(bf16[394,768]{1,0:T(8,128)(2,1)S(1)} %select_reduce_fusion.p_ref), custom_call_target="tpu_custom_call" | custom-call | tf_op jit(solution)/shard_map/tensor_sum/pallas_call | solution.py:74
  241.4 6.8 %gather_fusion.1 = f32[788,768]{1,0:T(8,128)} fusion(f32[1184,768]{1,0:T(8,128)} %reshape.302, s32[1024]{0:T(1024)S(1)} %pad_clamp_fusion), kind=kCustom, calls=%fused_computation.clone | custom fusion | bytes 4844624 | tf_op jit(solution)/shard_map/jit(_take)/gather | solution.py:518
  255.0 9.2 %psum.7 = bf16[394,2]{0,1:T(2,128)(2,1)S(1)} all-reduce(bf16[394,2]{0,1:T(2,128)(2,1)S(1)} %get-tuple-element.30), channel_id=1, replica_groups=mesh['dp'=32,'tensor'=4] {'tensor'}, use_global_device_ids=true, to_apply=%region_21.23 | all-reduce | flops 788 | bytes 3152 | tf_op jit(solution)/shard_map/psum | solution.py:584
  267.2 12.6 %tensor_sum.11 = bf16[394,768]{1,0:T(8,128)(2,1)S(1)} custom-call(bf16[394,768]{1,0:T(8,128)(2,1)S(1)} %get-tuple-element.31.p_ref), custom_call_target="tpu_custom_call" | custom-call | tf_op jit(solution)/shard_map/tensor_sum/pallas_call | solution.py:74
  292.7 13.5 %tensor_sum.13 = bf16[394,768]{1,0:T(8,128)(2,1)S(1)} custom-call(bf16[394,768]{1,0:T(8,128)(2,1)S(1)} %fusion.25.p_ref), custom_call_target="tpu_custom_call" | custom-call | tf_op jit(solution)/shard_map/tensor_sum/pallas_call | solution.py:74
  312.5 13.5 %tensor_sum.14 = bf16[394,768]{1,0:T(8,128)(2,1)S(1)} custom-call(bf16[394,768]{1,0:T(8,128)(2,1)S(1)} %convolution_convert_fusion.7.p_ref), custom_call_target="tpu_custom_call" | custom-call | tf_op jit(solution)/shard_map/tensor_sum/pallas_call | solution.py:74
  337.9 13.6 %tensor_sum.15 = bf16[394,768]{1,0:T(8,128)(2,1)S(1)} custom-call(bf16[394,768]{1,0:T(8,128)(2,1)S(1)} %fusion.26.p_ref), custom_call_target="tpu_custom_call" | custom-call | tf_op jit(solution)/shard_map/tensor_sum/pallas_call | solution.py:74
  370.4 77.7 %grad_sum.1 = (bf16[576,768]{1,0:T(8,128)(2,1)S(1)}, bf16[576,768]{1,0:T(8,128)(2,1)S(1)}, bf16[192,768]{1,0:T(8,128)(2,1)S(1)}, bf16[192,768]{1,0:T(8,128)(2,1)...) custom-call(bf16[576,768]{1,0:T(8,128)(2,1)S(1)} %bitcast.180, ...), custom_call_target="tpu_custom_call" | custom-call | tf_op jit(solution)/shard_map/grad_sum/pallas_call | solution.py:327
  (463 shorter events, 147.8 us)
Async XLA Ops:
  0.6 121.8 %copy-start = (bf16[1,768,768]{2,1,0:T(8,128)(2,1)S(1)}, bf16[1,768,768]{2,1,0:T(8,128)(2,1)}, u32[]{:S(2)}) copy-start(bf16[1,768,768]{2,1,0:T(8,128)(2,1)} %param.28) | copy-start | bytes 3538948
  6.1 19.4 %copy-start.83 = (f32[768]{0:T(1024)}, f32[768]{0:T(1024)S(1)}, u32[]{:S(2)}) copy-start(f32[768]{0:T(1024)S(1)} %get-tuple-element.103) | copy-start | bytes 9220
  6.1 19.4 %copy-start.120 = (f32[768]{0:T(1024)}, f32[768]{0:T(1024)S(1)}, u32[]{:S(2)}) copy-start(f32[768]{0:T(1024)S(1)} %get-tuple-element.48) | copy-start | bytes 9220
  6.1 40.7 %copy-start.79 = (f32[768]{0:T(1024)}, f32[768]{0:T(1024)S(1)}, u32[]{:S(2)}) copy-start(f32[768]{0:T(1024)S(1)} %get-tuple-element.101) | copy-start | bytes 9220
  6.1 40.7 %copy-start.118 = (f32[768]{0:T(1024)}, f32[768]{0:T(1024)S(1)}, u32[]{:S(2)}) copy-start(f32[768]{0:T(1024)S(1)} %get-tuple-element.50) | copy-start | bytes 9220
  6.1 69.4 %copy-start.85 = (f32[768]{0:T(1024)}, f32[768]{0:T(1024)S(1)}, u32[]{:S(2)}) copy-start(f32[768]{0:T(1024)S(1)} %get-tuple-element.104) | copy-start | bytes 9220
  24.8 21.3 %copy-start.1 = (bf16[394,768]{1,0:T(8,128)(2,1)}, bf16[394,768]{1,0:T(8,128)(2,1)S(1)}, u32[]{:S(2)}) copy-start(bf16[394,768]{1,0:T(8,128)(2,1)S(1)} %tensor_sum.8) | copy-start | bytes 1815556
  24.8 21.3 %copy-start.67 = (f32[768]{0:T(1024)}, f32[768]{0:T(1024)S(1)}, u32[]{:S(2)}) copy-start(f32[768]{0:T(1024)S(1)} %get-tuple-element.52) | copy-start | bytes 9220
  46.4 23.8 %copy-start.20 = (f32[394,768]{1,0:T(8,128)}, f32[394,768]{1,0:T(8,128)S(1)}, u32[]{:S(2)}) copy-start(f32[394,768]{1,0:T(8,128)S(1)} %get-tuple-element.70) | copy-start | bytes 3631108
  79.3 36.2 %all-to-all-start = ((bf16[32,37,768]{2,1,0:T(8,128)(2,1)}), bf16[32,37,768]{2,1,0:T(8,128)(2,1)S(1)}, u32[]{:S(2)}, u32[]{:S(2)}) async-start(bf16[32,37,768]{2,1,0:T(8,128)(2,1)} %reshape.285), calls=%async_computation | async-start | bytes 3932160 | tf_op jit(solution)/shard_map/all_to_all | solution.py:501
  115.5 32.1 %all-to-all-start.2 = ((bf16[32,37,768]{2,1,0:T(8,128)(2,1)}), bf16[32,37,768]{2,1,0:T(8,128)(2,1)}, u32[]{:S(2)}, u32[]{:S(2)}) async-start(bf16[32,37,768]{2,1,0:T(8,128)(2,1)} %reshape.289), calls=%async_computation.2 | async-start | bytes 3932160 | tf_op jit(solution)/shard_map/all_to_all | solution.py:555
  162.6 30.0 %all-to-all-start.3 = ((bf16[32,37,768]{2,1,0:T(8,128)(2,1)}), bf16[32,37,768]{2,1,0:T(8,128)(2,1)S(1)}, u32[]{:S(2)}, u32[]{:S(2)}) async-start(bf16[32,37,768]{2,1,0:T(8,128)(2,1)} %convolution_convert_fusion.1), calls=%async_computation.3 | async-start | bytes 3932160 | tf_op jit(solution)/shard_map/all_to_all | solution.py:572
  176.3 22.0 %copy-start.72 = (f32[2,3,197]{2,1,0:T(4,128)S(1)}, f32[2,3,197]{2,1,0:T(4,128)}, u32[]{:S(2)}) copy-start(f32[2,3,197]{2,1,0:T(4,128)} %copy-done.71) | copy-start | bytes 14188
  176.3 22.0 %copy-start.94 = (f32[2,3,197]{2,1,0:T(4,128)S(1)}, f32[2,3,197]{2,1,0:T(4,128)}, u32[]{:S(2)}) copy-start(f32[2,3,197]{2,1,0:T(4,128)} %copy-done.93) | copy-start | bytes 14188
  192.7 45.5 %all-to-all-start.1 = ((bf16[32,37,768]{2,1,0:T(8,128)(2,1)}), bf16[32,37,768]{2,1,0:T(8,128)(2,1)}, u32[]{:S(2)}, u32[]{:S(2)}) async-start(bf16[32,37,768]{2,1,0:T(8,128)(2,1)} %convolution_convert_fusion.2), calls=%async_computation.1 | async-start | bytes 3932160 | tf_op jit(solution)/shard_map/all_to_all | solution.py:508
  264.4 15.4 %copy-start.44 = (bf16[394,768]{1,0:T(8,128)(2,1)S(1)}, bf16[394,768]{1,0:T(8,128)(2,1)}, u32[]{:S(2)}) copy-start(bf16[394,768]{1,0:T(8,128)(2,1)} %param.18) | copy-start | bytes 1815556
  291.1 15.2 %copy-start.80 = (f32[768]{0:T(1024)S(1)}, f32[768]{0:T(1024)}, u32[]{:S(2)}) copy-start(f32[768]{0:T(1024)} %copy-done.79) | copy-start | bytes 9220
  291.1 15.2 %copy-start.88 = (f32[394]{0:T(512)S(1)}, f32[394]{0:T(512)}, u32[]{:S(2)}) copy-start(f32[394]{0:T(512)} %copy-done.87) | copy-start | bytes 4732
  291.1 15.2 %copy-start.98 = (f32[394]{0:T(512)S(1)}, f32[394]{0:T(512)}, u32[]{:S(2)}) copy-start(f32[394]{0:T(512)} %copy-done.97) | copy-start | bytes 4732
  308.0 18.9 %copy-start.38 = (f32[394,768]{1,0:T(8,128)}, f32[394,768]{1,0:T(8,128)S(1)}, u32[]{:S(2)}) copy-start(f32[394,768]{1,0:T(8,128)S(1)} %fusion.35) | copy-start | bytes 3631108
  310.0 16.0 %copy-start.68 = (f32[768]{0:T(1024)S(1)}, f32[768]{0:T(1024)}, u32[]{:S(2)}) copy-start(f32[768]{0:T(1024)} %copy-done.67) | copy-start | bytes 9220
  310.0 16.0 %copy-start.84 = (f32[768]{0:T(1024)S(1)}, f32[768]{0:T(1024)}, u32[]{:S(2)}) copy-start(f32[768]{0:T(1024)} %copy-done.83) | copy-start | bytes 9220
  310.0 16.0 %copy-start.96 = (f32[394]{0:T(512)S(1)}, f32[394]{0:T(512)}, u32[]{:S(2)}) copy-start(f32[394]{0:T(512)} %copy-done.95) | copy-start | bytes 4732
  310.0 16.1 %copy-start.104 = (f32[394]{0:T(512)S(1)}, f32[394]{0:T(512)}, u32[]{:S(2)}) copy-start(f32[394]{0:T(512)} %copy-done.103) | copy-start | bytes 4732
  (115 other events, 404.0 us)

commit v2 on v1

--- a/solution.py
+++ b/solution.py
@@ -478,124 +478,473 @@
     return (grad_out + grad_in, (in_part, out_part, gain_part, shift_part))
 
 
-def moe_forward(inputs, routes, router, expert_in, expert_out, ln_gain, ln_bias):
-    normed, normal, inverse = norm_forward(inputs, ln_gain[3], ln_bias[3])
-    normed_low = normed.astype(bfloat)
-    logits = jnp.dot(normed_low, router, preferred_element_type=single)
-    chosen = jnp.take_along_axis(logits, routes, axis=1)
-    gate_values = jax.nn.softmax(chosen, axis=1)
-    tokens_here, feature_width = normed_low.shape
-    expert_count = router.shape[1]
-    capacity = max(2, (3 * tokens_here + expert_count - 1) // expert_count)
-    one_hot = (routes[:, :, None] == jnp.arange(expert_count, dtype=jnp.int32)).astype(jnp.int32)
-    running = jnp.cumsum(one_hot.reshape(tokens_here * 2, expert_count), axis=0).reshape(
-        tokens_here, 2, expert_count
-    )
-    slot_index = routes * capacity + jnp.sum((running - 1) * one_hot, axis=-1)
-    slot_ids = jnp.arange(expert_count * capacity, dtype=jnp.int32)
-    dispatch_pair = (slot_ids[None, :, None] == slot_index.T[:, None, :]).astype(bfloat)
-    gathered = jnp.dot(
-        jnp.sum(dispatch_pair, axis=0), normed_low, preferred_element_type=single
-    ).astype(bfloat)
-    outgoing = gathered.reshape(expert_count, capacity, feature_width)
-    arrived_rows = lax.all_to_all(outgoing, "dp", split_axis=0, concat_axis=0, tiled=True)
-    sources = arrived_rows.shape[0]
-    items = arrived_rows.shape[1]
-    rows_flat = arrived_rows.reshape(sources * items, feature_width)
-    pre_rows = jnp.dot(rows_flat, expert_in[0], preferred_element_type=single)
-    act_rows = gelu_exact(pre_rows).astype(bfloat)
-    partial_out = jnp.dot(act_rows, expert_out[0], preferred_element_type=single)
-    back_rows = lax.all_to_all(
-        partial_out.reshape(sources, items, feature_width).astype(jnp.bfloat16),
-        "dp",
-        split_axis=0,
-        concat_axis=0,
-        tiled=True,
-    ).astype(jnp.float32)
-    hidden_width = pre_rows.shape[1]
-    pre_act = pre_rows.reshape(sources, items, hidden_width)
-    activated = act_rows.reshape(sources, items, hidden_width)
-    picked = jnp.take(back_rows.reshape(expert_count * capacity, feature_width), slot_index, axis=0)
-    mixed_part = jnp.sum(gate_values[:, :, None] * picked, axis=1)
-    mixed = tensor_sum(mixed_part.astype(jnp.bfloat16), 1).astype(jnp.float32)
-    stored = (
-        normal,
-        inverse,
-        normed_low,
-        gate_values,
-        slot_index,
-        dispatch_pair,
-        arrived_rows,
-        pre_act,
-        activated,
-        picked,
-    )
-    return (inputs + mixed, stored)
-
-
-def moe_backward(grad_out, routes, stored, router, expert_in, expert_out, ln_gain):
-    (
-        normal,
-        inverse,
-        normed_low,
-        gate_values,
-        slot_index,
-        dispatch_pair,
-        arrived,
-        pre_act,
-        activated,
-        picked,
-    ) = stored
-    expert_count, capacity, feature_width = arrived.shape
-    scaled = (gate_values[:, :, None] * grad_out[:, None, :]).astype(bfloat)
-    outgoing = jnp.einsum(
-        "kst,tkd->sd", dispatch_pair, scaled, preferred_element_type=single
-    ).astype(bfloat)
-    gate_part = jnp.sum(picked * grad_out[:, None, :], axis=-1)
-    arrived_grad = lax.all_to_all(
-        outgoing.reshape(expert_count, capacity, feature_width),
-        "dp",
-        split_axis=0,
-        concat_axis=0,
-        tiled=True,
-    )
-    row_count = expert_count * capacity
-    rows_grad = arrived_grad.reshape(row_count, feature_width)
-    flat_rows = arrived.reshape(row_count, feature_width)
-    flat_pre = pre_act.reshape(row_count, pre_act.shape[2])
-    flat_act = activated.reshape(row_count, activated.shape[2])
-    expert_out_part = jnp.einsum("sf,sd->fd", flat_act, rows_grad, preferred_element_type=single)
-    grad_act = jnp.einsum("sd,fd->sf", rows_grad, expert_out[0], preferred_element_type=single)
-    grad_pre = gelu_slope(flat_pre, grad_act).astype(bfloat)
-    expert_in_part = jnp.einsum("sd,sf->df", flat_rows, grad_pre, preferred_element_type=single)
-    rows_back = jnp.einsum("sf,df->sd", grad_pre, expert_in[0], preferred_element_type=single)
-    returned = lax.all_to_all(
-        rows_back.reshape(expert_count, capacity, feature_width).astype(jnp.bfloat16),
-        "dp",
-        split_axis=0,
-        concat_axis=0,
-        tiled=True,
-    ).astype(jnp.float32)
-    normed_part = jnp.sum(
-        jnp.take(returned.reshape(row_count, feature_width), slot_index, axis=0), axis=1
-    )
-    grad_experts, grad_gates = (
-        tensor_sum(normed_part.astype(jnp.bfloat16), 1).astype(jnp.float32),
-        lax.psum(gate_part.astype(jnp.bfloat16), "tensor").astype(jnp.float32),
-    )
+EXPERTS = 32
+STRIDE = 40
+SLOTS = EXPERTS * STRIDE
+
+
+def dot_rows(a, b):
+    return lax.dot_general(a, b, (((1,), (0,)), ((), ())), preferred_element_type=single)
+
+
+def dot_last(a, b):
+    return lax.dot_general(a, b, (((1,), (1,)), ((), ())), preferred_element_type=single)
+
+
+def dot_first(a, b):
+    return lax.dot_general(a, b, (((0,), (0,)), ((), ())), preferred_element_type=single)
+
+
+def moe_route_kernel(
+    rows_ref, cotangent_ref, routes_ref, routes_row_ref, router_ref, gain_ref, shift_ref,
+    out_ref, low_ref, normal_ref, inverse_ref, gates_ref, slots_ref,
+):
+    tokens, width = rows_ref.shape
+    half = width // 2
+    normed, normal, inverse = norm_forward(rows_ref[...], gain_ref[...], shift_ref[...])
+    low = normed.astype(bfloat)
+    low_ref[...] = low
+    normal_ref[...] = normal
+    inverse_ref[...] = inverse
+    logits = dot_last(low, router_ref[...])
+    experts = lax.broadcasted_iota(jnp.int32, (tokens, EXPERTS), 1)
+    picks = [routes_ref[:, k : k + 1] == experts for k in range(2)]
+    chosen = [jnp.sum(jnp.where(pick, logits, 0.0), axis=1, keepdims=True) for pick in picks]
+    largest = jnp.maximum(chosen[0], chosen[1])
+    powers = [jnp.exp(c - largest) for c in chosen]
+    total = powers[0] + powers[1]
+    gates = [power / total for power in powers]
+    gates_ref[:, 0:1] = gates[0]
+    gates_ref[:, 1:2] = gates[1]
+
+    before = lax.broadcasted_iota(jnp.int32, (tokens, tokens), 0)
+    after = lax.broadcasted_iota(jnp.int32, (tokens, tokens), 1)
+    either = [jnp.where(pick, 1.0, 0.0) for pick in picks]
+    lower = jnp.where(after < before, 1.0, 0.0).astype(bfloat)
+    running = dot_rows(lower, (either[0] + either[1]).astype(bfloat))
+    for k in range(2):
+        rank = jnp.sum(running * either[k], axis=1, keepdims=True).astype(jnp.int32)
+        slots_ref[:, k : k + 1] = routes_ref[:, k : k + 1] * STRIDE + rank
+
+    experts_row = lax.broadcasted_iota(jnp.int32, (EXPERTS, tokens), 0)
+    either_row = [
+        jnp.where(routes_row_ref[k : k + 1, :] == experts_row, 1.0, 0.0) for k in range(2)
+    ]
+    upper = jnp.where(before < after, 1.0, 0.0).astype(bfloat)
+    running_row = dot_rows((either_row[0] + either_row[1]).astype(bfloat), upper)
+    slots_row = []
+    for k in range(2):
+        rank = jnp.sum(running_row * either_row[k], axis=0, keepdims=True).astype(jnp.int32)
+        slots_row.append(routes_row_ref[k : k + 1, :] * STRIDE + rank)
+
+    cotangent = cotangent_ref[...].astype(single)
+    scaled = [(gate * cotangent).astype(bfloat) for gate in gates]
+    block = SLOTS // 8
+    for i in range(8):
+        ids = lax.broadcasted_iota(jnp.int32, (block, tokens), 0) + i * block
+        hits = [jnp.where(ids == slots_row[k], 1.0, 0.0) for k in range(2)]
+        moved = dot_rows((hits[0] + hits[1]).astype(bfloat), low).astype(bfloat)
+        moved_grad = (
+            dot_rows(hits[0].astype(bfloat), scaled[0]) + dot_rows(hits[1].astype(bfloat), scaled[1])
+        ).astype(bfloat)
+        at = slice(i * block, (i + 1) * block)
+        for h in range(2):
+            out_ref[h, at, :half] = moved[:, h * half : (h + 1) * half]
+            out_ref[h, at, half:] = moved_grad[:, h * half : (h + 1) * half]
+
+
+VMEM_SPEC = pl.BlockSpec(memory_space=pltpu.VMEM)
+
+
+def moe_route(rows, cotangent, routes, router, gain_row, shift_row):
+    tokens, width = rows.shape
+    shapes = [
+        jax.ShapeDtypeStruct((2, SLOTS, width), bfloat),
+        jax.ShapeDtypeStruct((tokens, width), bfloat),
+        jax.ShapeDtypeStruct((tokens, width), single),
+        jax.ShapeDtypeStruct((tokens, 1), single),
+        jax.ShapeDtypeStruct((tokens, 2), single),
+        jax.ShapeDtypeStruct((tokens, 2), jnp.int32),
+    ]
+    return pl.pallas_call(
+        moe_route_kernel,
+        out_shape=shapes,
+        in_specs=[VMEM_SPEC] * 7,
+        out_specs=[VMEM_SPEC] * 6,
+        compiler_params=pltpu.CompilerParams(vmem_limit_bytes=48 * 2**20),
+        name="moe_route",
+    )(rows, cotangent, routes, routes.T, router.T, gain_row[None], shift_row[None])
+
+
+def dp_peer(k):
+    dp = lax.axis_index("dp")
+    plane = lax.rem(dp // 16 + k // 16, 2)
+    x = lax.rem(lax.rem(dp // 4, 4) + lax.rem(k // 4, 4), 4)
+    y = lax.rem(lax.rem(dp, 4) + lax.rem(k, 4), 4)
+    return plane * 16 + x * 4 + y
+
+
+def dp_source(k):
+    dp = lax.axis_index("dp")
+    plane = lax.rem(dp // 16 + k // 16, 2)
+    x = lax.rem(lax.rem(dp // 4, 4) + 4 - lax.rem(k // 4, 4), 4)
+    y = lax.rem(lax.rem(dp, 4) + 4 - lax.rem(k, 4), 4)
+    return plane * 16 + x * 4 + y
+
+
+def order_of(i):
+    return lax.rem(i * 11, EXPERTS)
+
+
+def meet_all(sibling):
+    barrier = pltpu.get_barrier_semaphore()
+
+    def greet(k, carry):
+        pl.semaphore_signal(barrier, inc=1, device_id={"dp": dp_peer(k)}, device_id_type=MESH)
+        return carry
+
+    lax.fori_loop(1, EXPERTS, greet, 0)
+    pl.semaphore_signal(barrier, inc=1, device_id=sibling, device_id_type=MESH)
+    pl.semaphore_wait(barrier, EXPERTS)
+
+
+def moe_send_kernel(in_ref, out_ref, local_sem, send_sem, recv_sem, pass_sem, land_sem):
+    t = lax.axis_index("tensor")
+    dp = lax.axis_index("dp")
+    core = lax.rem(t, 2)
+    sibling = {"tensor": t + 1 - 2 * core}
+    own = pltpu.make_async_copy(in_ref.at[core, dp], out_ref.at[core, dp], local_sem)
+    own.start()
+    meet_all(sibling)
+
+    def across(k):
+        peer = dp_peer(k)
+        return pltpu.make_async_remote_copy(
+            src_ref=in_ref.at[core, peer],
+            dst_ref=out_ref.at[core, dp],
+            send_sem=send_sem.at[k],
+            recv_sem=recv_sem.at[k],
+            device_id={"dp": peer},
+            device_id_type=MESH,
+        )
+
+    def beside(k):
+        block = out_ref.at[core, dp_source(k)]
+        return pltpu.make_async_remote_copy(
+            src_ref=block,
+            dst_ref=block,
+            send_sem=pass_sem.at[k],
+            recv_sem=land_sem.at[k],
+            device_id=sibling,
+            device_id_type=MESH,
+        )
+
+    def start(i, carry):
+        across(order_of(i)).start()
+        return carry
+
+    def forward(i, carry):
+        k = order_of(i)
+        across(k).wait_recv()
+        beside(k).start()
+        return carry
+
+    def land(k, carry):
+        beside(k).wait_recv()
+        return carry
+
+    def drain(k, carry):
+        across(k).wait_send()
+        return carry
+
+    def drain_pass(k, carry):
+        beside(k).wait_send()
+        return carry
+
+    lax.fori_loop(1, EXPERTS, start, 0)
+    own.wait()
+    beside(0).start()
+    lax.fori_loop(1, EXPERTS, forward, 0)
+    lax.fori_loop(0, EXPERTS, land, 0)
+    lax.fori_loop(1, EXPERTS, drain, 0)
+    lax.fori_loop(0, EXPERTS, drain_pass, 0)
+
+
+def moe_send(rows, collective_id):
+    every = pltpu.SemaphoreType.DMA((EXPERTS,))
+    hbm = pl.BlockSpec(memory_space=pl.ANY)
+    return pl.pallas_call(
+        moe_send_kernel,
+        out_shape=jax.ShapeDtypeStruct(rows.shape, bfloat),
+        in_specs=[hbm],
+        out_specs=hbm,
+        scratch_shapes=[pltpu.SemaphoreType.DMA, every, every, every, every],
+        compiler_params=pltpu.CompilerParams(collective_id=collective_id, has_side_effects=True),
+        name="moe_send",
+    )(rows)
+
+
+def expert_kernel(in_ref, ein_ref, eout_ref, out_ref, ein_grad_ref, eout_grad_ref, act_ref, grad_ref):
+    half = in_ref.shape[2] // 2
+    width = 2 * half
+    block = SLOTS // 4
+
+    def both(at, first):
+        parts = [in_ref[h, at, first : first + half] for h in range(2)]
+        return jnp.concatenate(parts, axis=1)
+
+    def forward(i, carry):
+        at = pl.ds(pl.multiple_of(i * block, 16), block)
+        rows = both(at, 0)
+        rows_grad = both(at, half)
+        pre = dot_rows(rows, ein_ref[0])
+        grad_act = dot_last(rows_grad, eout_ref[0])
+        tail = 0.5 * (1.0 + lax.erf(pre * (0.5**0.5)))
+        act = (pre * tail).astype(bfloat)
+        slope = tail + pre * (jnp.exp(-0.5 * pre * pre) * 0.3989422804014327)
+        grad_pre = (grad_act * slope).astype(bfloat)
+        act_ref[at, :] = act
+        grad_ref[at, :] = grad_pre
+        out = dot_rows(act, eout_ref[0]).astype(bfloat)
+        back = dot_last(grad_pre, ein_ref[0]).astype(bfloat)
+        for h in range(2):
+            out_ref[h, at, :half] = out[:, h * half : (h + 1) * half]
+            out_ref[h, at, half:] = back[:, h * half : (h + 1) * half]
+        return carry
+
+    lax.fori_loop(0, SLOTS // block, forward, 0)
+    for h in range(2):
+        eout_grad_ref[0, :, h * half : (h + 1) * half] = dot_first(act_ref[...], in_ref[h, :, half:])
+        ein_grad_ref[0, h * half : (h + 1) * half, :] = dot_first(in_ref[h, :, :half], grad_ref[...])
+
+
+def expert_ffn(rows, expert_in, expert_out):
+    width = rows.shape[2]
+    weight = jax.ShapeDtypeStruct(expert_in.shape, single)
+    return pl.pallas_call(
+        expert_kernel,
+        out_shape=[jax.ShapeDtypeStruct(rows.shape, bfloat), weight, weight],
+        in_specs=[VMEM_SPEC] * 3,
+        out_specs=[VMEM_SPEC] * 3,
+        scratch_shapes=[pltpu.VMEM((SLOTS, width), bfloat)] * 2,
+        compiler_params=pltpu.CompilerParams(vmem_limit_bytes=56 * 2**20),
+        name="expert_ffn",
+    )(rows, expert_in, expert_out)
+
+
+def moe_return_kernel(in_ref, out_ref, got_ref, sum_ref, local_sem, send_sem, recv_sem, pass_sem, land_sem):
+    t = lax.axis_index("tensor")
+    dp = lax.axis_index("dp")
+    core = lax.rem(t, 2)
+    sibling = {"tensor": t + 1 - 2 * core}
+    meet_all(sibling)
+
+    def beside(k):
+        peer = dp_peer(k)
+        return pltpu.make_async_remote_copy(
+            src_ref=in_ref.at[1 - core, peer],
+            dst_ref=got_ref.at[peer],
+            send_sem=pass_sem.at[k],
+            recv_sem=land_sem.at[k],
+            device_id=sibling,
+            device_id_type=MESH,
+        )
+
+    def across(k):
+        peer = dp_peer(k)
+        return pltpu.make_async_remote_copy(
+            src_ref=sum_ref.at[peer],
+            dst_ref=out_ref.at[dp],
+            send_sem=send_sem.at[k],
+            recv_sem=recv_sem.at[k],
+            device_id={"dp": peer},
+            device_id_type=MESH,
+        )
+
+    def start(i, carry):
+        beside(order_of(i)).start()
+        return carry
+
+    def combine(i, carry):
+        k = order_of(i)
+        peer = dp_peer(k)
+        beside(k).wait_recv()
+        total = in_ref[core, peer].astype(single) + got_ref[peer].astype(single)
+        sum_ref[peer] = total.astype(bfloat)
+        return k
+
+    def onward(i, carry):
+        k = combine(i, carry)
+        across(k).start()
+        return carry
+
+    def arrive(k, carry):
+        across(k).wait_recv()
+        return carry
+
+    def drain(k, carry):
+        across(k).wait_send()
+        return carry
+
+    def drain_pass(k, carry):
+        beside(k).wait_send()
+        return carry
+
+    lax.fori_loop(1, EXPERTS + 1, start, 0)
+    lax.fori_loop(1, EXPERTS, onward, 0)
+    combine(EXPERTS, 0)
+    own = pltpu.make_async_copy(sum_ref.at[dp], out_ref.at[dp], local_sem)
+    own.start()
+    lax.fori_loop(1, EXPERTS, arrive, 0)
+    lax.fori_loop(1, EXPERTS, drain, 0)
+    lax.fori_loop(0, EXPERTS, drain_pass, 0)
+    own.wait()
+
+
+def moe_return(rows, collective_id):
+    every = pltpu.SemaphoreType.DMA((EXPERTS,))
+    block = pltpu.VMEM(rows.shape[1:], bfloat)
+    return pl.pallas_call(
+        moe_return_kernel,
+        out_shape=jax.ShapeDtypeStruct(rows.shape[1:], bfloat),
+        in_specs=[VMEM_SPEC],
+        out_specs=pl.BlockSpec(memory_space=pl.ANY),
+        scratch_shapes=[block, block, pltpu.SemaphoreType.DMA, every, every, every, every],
+        compiler_params=pltpu.CompilerParams(
+            collective_id=collective_id, has_side_effects=True, vmem_limit_bytes=32 * 2**20
+        ),
+        name="moe_return",
+    )(rows)
+
+
+def combine_kernel(back_ref, slots_ref, gates_ref, cotangent_ref, out_ref):
+    tokens = slots_ref.shape[0]
+    half = back_ref.shape[1] // 2
+    core = lax.rem(lax.axis_index("tensor"), 2)
+    own = cotangent_ref[:, pl.ds(pl.multiple_of(core * half, 128), half)].astype(single)
+    ids = lax.broadcasted_iota(jnp.int32, (tokens, SLOTS), 1)
+    hits = [jnp.where(ids == slots_ref[:, k : k + 1], 1.0, 0.0) for k in range(2)]
+    picked = [dot_rows(hit.astype(bfloat), back_ref[:, :half]) for hit in hits]
+    mixed = gates_ref[:, 0:1] * picked[0] + gates_ref[:, 1:2] * picked[1]
+    gate = [jnp.sum(p * own, axis=1, keepdims=True) for p in picked]
+    normed = dot_rows((hits[0] + hits[1]).astype(bfloat), back_ref[:, half:])
+    for j in range(half // 128):
+        out_ref[j] = mixed[:, j * 128 : (j + 1) * 128].astype(bfloat)
+        out_ref[half // 128 + j] = normed[:, j * 128 : (j + 1) * 128].astype(bfloat)
+    lane = lax.broadcasted_iota(jnp.int32, (tokens, 128), 1)
+    spread = jnp.where(lane == 0, gate[0], jnp.where(lane == 1, gate[1], 0.0))
+    out_ref[2 * (half // 128)] = spread.astype(bfloat)
+
+
+def combine(back, slots, gates, cotangent):
+    tokens = slots.shape[0]
+    return pl.pallas_call(
+        combine_kernel,
+        out_shape=jax.ShapeDtypeStruct((7, tokens, 128), bfloat),
+        in_specs=[VMEM_SPEC] * 4,
+        out_specs=VMEM_SPEC,
+        compiler_params=pltpu.CompilerParams(vmem_limit_bytes=48 * 2**20),
+        name="combine",
+    )(back, slots, gates, cotangent)
+
+
+def combine_sum_kernel(p_ref, mixed_ref, normed_ref, gates_ref, got_two, sum_two, got_three, sems):
+    t = lax.axis_index("tensor")
+    core = lax.rem(t, 2)
+    sibling = {"tensor": t + 1 - 2 * core}
+    opposite = {"tensor": lax.rem(t + 2, 4)}
+    barrier = pltpu.get_barrier_semaphore()
+    for peer in (sibling, opposite):
+        pl.semaphore_signal(barrier, inc=1, device_id=peer, device_id_type=MESH)
+    pl.semaphore_wait(barrier, 2)
+
+    def copy(source, target, step, j, peer):
+        return pltpu.make_async_remote_copy(
+            src_ref=source,
+            dst_ref=target,
+            send_sem=sems.at[0, step, j],
+            recv_sem=sems.at[1, step, j],
+            device_id=peer,
+            device_id_type=MESH,
+        )
+
+    count = p_ref.shape[0]
+    order = [6, 0, 1, 2, 3, 4, 5]
+    second = [copy(p_ref.at[j], got_two.at[j], 0, j, opposite) for j in range(count)]
+    third = [copy(sum_two.at[j], got_three.at[j], 1, j, sibling) for j in range(count)]
+    for j in order:
+        second[j].start()
+
+    def place(j, which):
+        ref = mixed_ref if j < 3 else normed_ref
+        return ref, pl.ds(pl.multiple_of((which * 3 + j % 3) * 128, 128), 128)
+
+    for j in order:
+        second[j].wait_recv()
+        whole = (p_ref[j].astype(single) + got_two[j].astype(single)).astype(bfloat)
+        sum_two[j] = whole
+        third[j].start()
+        if j < 6:
+            ref, at = place(j, core)
+            ref[:, at] = whole
+    for j in order:
+        third[j].wait_recv()
+        if j < 6:
+            ref, at = place(j, 1 - core)
+            ref[:, at] = got_three[j]
+        else:
+            gates_ref[...] = sum_two[j].astype(single) + got_three[j].astype(single)
+    for j in range(count):
+        second[j].wait_send()
+        third[j].wait_send()
+
+
+def combine_sum(parts, collective_id):
+    count, tokens, lanes = parts.shape
+    block = pltpu.VMEM(parts.shape, bfloat)
+    whole = jax.ShapeDtypeStruct((tokens, 768), bfloat)
+    return pl.pallas_call(
+        combine_sum_kernel,
+        out_shape=[whole, whole, jax.ShapeDtypeStruct((tokens, lanes), single)],
+        in_specs=[VMEM_SPEC],
+        out_specs=[VMEM_SPEC] * 3,
+        scratch_shapes=[block] * 3 + [pltpu.SemaphoreType.DMA((2, 2, count))],
+        compiler_params=pltpu.CompilerParams(
+            collective_id=collective_id, has_side_effects=True, vmem_limit_bytes=32 * 2**20
+        ),
+        name="combine_sum",
+    )(parts)
+
+
+def moe_block(inputs, cotangent, routes, router, expert_in, expert_out, ln_gain, ln_bias):
+    tokens_here, feature_width = inputs.shape
+    sent, normed_low, normal, inverse, gate_values, slots = moe_route(
+        inputs, cotangent, routes, router, ln_gain[3], ln_bias[3]
+    )
+    arrived = moe_send(sent.reshape(2, EXPERTS, STRIDE, feature_width), 3)
+    answers, expert_in_grad, expert_out_grad = expert_ffn(
+        arrived.reshape(2, SLOTS, feature_width), expert_in, expert_out
+    )
+    returned = moe_return(answers.reshape(2, EXPERTS, STRIDE, feature_width), 4)
+    parts = combine(returned.reshape(SLOTS, feature_width), slots, gate_values, cotangent)
+    mixed, grad_experts, gate_sums = combine_sum(parts, 5)
+    output = (inputs + mixed.astype(single)).astype(bfloat)
+    grad_out = cotangent.astype(single)
+    grad_gates = gate_sums[:, :2]
     grad_chosen = gate_values * (
         grad_gates - jnp.sum(gate_values * grad_gates, axis=1, keepdims=True)
     )
     one_hot = (routes[:, :, None] == jnp.arange(router.shape[1], dtype=jnp.int32)).astype(single)
     grad_logits = jnp.sum(one_hot * grad_chosen[:, :, None], axis=1).astype(bfloat)
     router_part = jnp.einsum("td,te->de", normed_low, grad_logits, preferred_element_type=single)
-    grad_normed = grad_experts + jnp.einsum(
+    grad_normed = grad_experts.astype(single) + jnp.einsum(
         "te,de->td", grad_logits, router, preferred_element_type=single
     )
     grad_in, gain_part, shift_part = norm_backward(grad_normed, normal, inverse, ln_gain[3])
     return (
+        output,
         grad_out + grad_in,
-        (router_part, expert_in_part[None], expert_out_part[None], gain_part, shift_part),
+        (router_part, expert_in_grad, expert_out_grad, gain_part, shift_part),
     )
 
 
@@ -623,13 +972,8 @@
     section_three, stored_two = attend_forward(
         section_two, 1, qkv_weight, out_weight, qv_bias, out_bias, ln_gain, ln_bias
     )
-    section_four, stored_moe = moe_forward(
-        section_three, routes, router, expert_in, expert_out, ln_gain, ln_bias
-    )
-    output = section_four.astype(bfloat)
-    grad_four = cotangent.astype(single)
-    grad_three, moe_parts = moe_backward(
-        grad_four, routes, stored_moe, router, expert_in, expert_out, ln_gain
+    output, grad_three, moe_parts = moe_block(
+        section_three, cotangent, routes, router, expert_in, expert_out, ln_gain, ln_bias
     )
     router_grad, expert_in_grad, expert_out_grad, gain_three, shift_three = moe_parts
     grad_two, upper_parts = attend_backward(

time: 466 us -> 379 us (0.81)
  Pallas kernels: 186 us -> 273 us
  local copies, waits for them, and re-layouts: 95.2 us -> 38.4 us
  matrix products: 74.6 us -> 34.3 us
  waiting for transfers between devices: 34.9 us -> 0 us
  starting transfers between devices: 25.5 us -> 0 us
  blocking collectives: 9.23 us -> 0 us
  other arithmetic: 31.6 us -> 25.2 us
    pallas_call x0 -> x6, Pallas kernels: none -> 115 us  [the longest x1 37 us: moe_send(): pl.pallas_call(moe_send_kernel, out_shape=jax.ShapeDtypeStruct(rows.shape...]
    dot_general x11 -> x2, matrix products: 46.3 us -> 3.17 us  [the longest x1 1.91 us: moe_block(): jnp.einsum('te,de->td', grad_logits, router, preferred_element_type=single)]
    all_to_all x4 -> x0, waiting for transfers between devices: 34.9 us -> none  [the longest x1 16.3 us: moe_backward(): lax.all_to_all(rows_back.reshape(expert_count, capacity, feature_width).a...]
    gather x9 -> x0, local copies, waits for them, and re-layouts: 32.9 us -> none  [the longest x5 11.2 us: moe_forward(): chosen = jnp.take_along_axis(logits, routes, axis=1)]
    pallas_call x8 -> x6, Pallas kernels: 108 us -> 81.6 us  [tensor_sum(): pl.pallas_call(functools.partial(tensor_sum_kernel, count, rows), out_sha...]
    all_to_all x4 -> x0, starting transfers between devices: 25.5 us -> none  [the longest x1 8.94 us: moe_forward(): lax.all_to_all(outgoing, 'dp', split_axis=0, concat_axis=0, tiled=True)]
    reshape x6 -> x0, local copies, waits for them, and re-layouts: 12.9 us -> none  [the longest x1 3.22 us: moe_forward(): back_rows.reshape(expert_count * capacity, feature_width)]
    psum x1 -> x0, blocking collectives: 9.23 us -> none  [moe_backward(): lax.psum(gate_part.astype(jnp.bfloat16), 'tensor').astype(jnp.float32)]
  transfers between devices with their start and end apart: 4 -> 0, of which waited for: 3 -> 0; matrix products, arithmetic and copies ran while one was open for 15% -> 0% of each run, Pallas kernels for 3% -> 0%
where the time goes in v2:
time: 379 us; the launch traced here: 374 us
  Pallas kernels  273 us (72%)
  local copies, waits for them, and re-layouts  38.4 us (10%)
  matrix products  34.3 us (9%)
  other arithmetic  25.2 us (7%)
    pallas_call x6, Pallas kernels, tensor_sum(): pl.pallas_call(functools.partial(tensor_sum_kernel, count, rows), out_sha...  81.6 us
    pallas_call x1, Pallas kernels, grad_sum(): pl.pallas_call(grad_sum_kernel, out_shape=[jax.ShapeDtypeStruct(a.shape,...  76.8 us
    pallas_call x1, Pallas kernels, moe_send(): pl.pallas_call(moe_send_kernel, out_shape=jax.ShapeDtypeStruct(rows.shape...  37 us
    pallas_call x1, Pallas kernels, moe_return(): pl.pallas_call(moe_return_kernel, out_shape=jax.ShapeDtypeStruct(rows.sha...  32.1 us
    pallas_call x1, Pallas kernels, combine_sum(): pl.pallas_call(combine_sum_kernel, out_shape=[whole, whole, jax.ShapeDtyp...  21 us
    unnamed x207, local copies, waits for them, and re-layouts  19.2 us
    pallas_call x1, Pallas kernels, expert_ffn(): pl.pallas_call(expert_kernel, out_shape=[jax.ShapeDtypeStruct(rows.shape,...  16 us

profile of v2, /device:TPU:0, one launch (start us, length us, event | category | flops | bytes accessed | tf_op | source)
XLA Modules:
  0.0 373.6 jit_solution(16202365253270591195)
XLA Ops:
  4.7 2.5 fusion.118
  11.5 14.0 %tensor_sum.6 = bf16[394,768]{1,0:T(8,128)(2,1)S(1)} custom-call(bf16[394,768]{1,0:T(8,128)(2,1)S(1)} %convolution_convert_fusion.7.p_ref), custom_call_target="tpu_custom_call" | custom-call | tf_op jit(solution)/shard_map/tensor_sum/pallas_call | solution.py:74
  26.2 4.6 %multiply_convert_fusion.2 = (bf16[394,768]{1,0:T(8,128)(2,1)S(1)}, f32[394,768]{1,0:T(8,128)}, f32[394,768]{1,0:T(8,128)}) fusion(bf16[768,768]{1,0:T(8,128)(2,1)S(1)} %copy-done, f32[768]{0:T(1024)S(1)} %get-tuple-element.69, f32[768]{0:T(1024)S(1)} %get-tuple-element.116, f32[394]{0:T(512)S(1)} %add_rsqrt_fusion.1, f32[394]{0:T(512)S(1)} %broadcast_multiply_fusion.9, ...), kind=kOutput, calls=%fused_computation.76 | convolution fusion | flops 487173120 | bytes 5428304 | tf_op jit(solution)/shard_map/dot_general | solution.py:461
  31.7 13.5 %tensor_sum.7 = bf16[394,768]{1,0:T(8,128)(2,1)S(1)} custom-call(bf16[394,768]{1,0:T(8,128)(2,1)S(1)} %convolution_convert_fusion.6.p_ref), custom_call_target="tpu_custom_call" | custom-call | tf_op jit(solution)/shard_map/tensor_sum/pallas_call | solution.py:74
  54.8 13.6 %tensor_sum.8 = bf16[394,768]{1,0:T(8,128)(2,1)S(1)} custom-call(bf16[394,768]{1,0:T(8,128)(2,1)S(1)} %convolution_convert_fusion.5.p_ref), custom_call_target="tpu_custom_call" | custom-call | tf_op jit(solution)/shard_map/tensor_sum/pallas_call | solution.py:74
  69.5 6.5 %moe_route.1 = (bf16[2,1280,768]{2,1,0:T(8,128)(2,1)}, bf16[394,768]{1,0:T(8,128)(2,1)S(1)}, f32[394,768]{1,0:T(8,128)S(1)}, f32[394,1]{1,0:T(8,128)S(1)}, f32[394,2]{1,0:T(8,128)S(1)}, /*index=5*/s32[394,2]{1,0:T(8,128)S(1)}) custom-call(f32[394,768]{1,0:T(8,128)S(1)} %add_add_fusion.rows_ref, bf16[394,768]{1,0:T(8,128)(2,1)S(1)} %copy-done.1, ...), custom_call_target="tpu_custom_call" | custom-call | tf_op jit(solution)/shard_map/moe_route/pallas_call | solution.py:569
  79.2 37.0 %moe_send.1 = bf16[2,32,40,768]{3,2,1,0:T(8,128)(2,1)} custom-call(bf16[2,32,40,768]{3,2,1,0:T(8,128)(2,1)} %bitcast.141), custom_call_target="tpu_custom_call" | custom-call | tf_op jit(solution)/shard_map/moe_send/pallas_call | solution.py:676
  116.9 16.0 %expert_ffn.1 = (bf16[2,1280,768]{2,1,0:T(8,128)(2,1)}, f32[1,768,768]{2,1,0:T(8,128)}, f32[1,768,768]{2,1,0:T(8,128)}) custom-call(bf16[2,1280,768]{2,1,0:T(8,128)(2,1)} %bitcast.140, bf16[1,768,768]{2,1,0:T(8,128)(2,1)} %ein_ref.1, bf16[1,768,768]{2,1,0:T(8,128)(2,1)} %eout_ref.1), custom_call_target="tpu_custom_call" | custom-call | tf_op jit(solution)/shard_map/expert_ffn/pallas_call | solution.py:724
  133.0 2.1 copy-done.6
  135.1 32.1 %moe_return.1 = bf16[32,40,768]{2,1,0:T(8,128)(2,1)S(1)} custom-call(bf16[2,32,40,768]{3,2,1,0:T(8,128)(2,1)S(1)} %bitcast.131), custom_call_target="tpu_custom_call" | custom-call | tf_op jit(solution)/shard_map/moe_return/pallas_call | solution.py:807
  167.2 2.3 combine.1.p_ref
  169.4 21.0 %combine_sum.1 = (bf16[394,768]{1,0:T(8,128)(2,1)S(1)}, bf16[394,768]{1,0:T(8,128)(2,1)S(1)}, f32[394,128]{1,0:T(8,128)S(1)}) custom-call(bf16[7,394,128]{2,1,0:T(8,128)(2,1)S(1)} %combine.1.p_ref), custom_call_target="tpu_custom_call" | custom-call | tf_op jit(solution)/shard_map/combine_sum/pallas_call | solution.py:906
  194.9 1.9 multiply_reduce_fusion
  209.1 13.6 %tensor_sum.9 = bf16[394,768]{1,0:T(8,128)(2,1)S(1)} custom-call(bf16[394,768]{1,0:T(8,128)(2,1)S(1)} %fusion.13.p_ref), custom_call_target="tpu_custom_call" | custom-call | tf_op jit(solution)/shard_map/tensor_sum/pallas_call | solution.py:74
  222.8 2.1 fusion.25
  225.0 1.9 fusion.23
  232.7 13.6 %tensor_sum.10 = bf16[394,768]{1,0:T(8,128)(2,1)S(1)} custom-call(bf16[394,768]{1,0:T(8,128)(2,1)S(1)} %convolution_convert_fusion.4.p_ref), custom_call_target="tpu_custom_call" | custom-call | tf_op jit(solution)/shard_map/tensor_sum/pallas_call | solution.py:74
  248.8 2.0 convolution_convert_fusion.1.refs_4_
  262.2 13.5 %tensor_sum.11 = bf16[394,768]{1,0:T(8,128)(2,1)S(1)} custom-call(bf16[394,768]{1,0:T(8,128)(2,1)S(1)} %fusion.14.p_ref), custom_call_target="tpu_custom_call" | custom-call | tf_op jit(solution)/shard_map/tensor_sum/pallas_call | solution.py:74
  276.7 1.9 concatenate.6.refs_6_
  278.6 2.9 fusion.19
  283.3 76.8 %grad_sum.1 = (bf16[576,768]{1,0:T(8,128)(2,1)S(1)}, bf16[576,768]{1,0:T(8,128)(2,1)S(1)}, bf16[192,768]{1,0:T(8,128)(2,1)S(1)}, bf16[192,768]{1,0:T(8,128)(2,1)...) custom-call(bf16[576,768]{1,0:T(8,128)(2,1)S(1)} %bitcast.133, ...), custom_call_target="tpu_custom_call" | custom-call | tf_op jit(solution)/shard_map/grad_sum/pallas_call | solution.py:327
  365.9 2.3 maximum_convert_fusion
  368.2 2.0 convert_bitcast_fusion
  (339 shorter events, 71.7 us)
Async XLA Ops:
  0.6 25.5 %copy-start = (bf16[768,768]{1,0:T(8,128)(2,1)S(1)}, bf16[768,768]{1,0:T(8,128)(2,1)}, u32[]{:S(2)}) copy-start(bf16[768,768]{1,0:T(8,128)(2,1)} %param.23) | copy-start | bytes 3538948
  2.0 5.2 %copy-start.64 = (f32[394]{0:T(512)}, f32[394]{0:T(512)S(1)}, u32[]{:S(2)}) copy-start(f32[394]{0:T(512)S(1)} %broadcast_multiply_fusion.10) | copy-start | bytes 4732
  3.6 48.6 %copy-start.83 = (f32[3,64]{1,0:T(4,128)}, f32[3,64]{1,0:T(4,128)S(1)}, u32[]{:S(2)}) copy-start(f32[3,64]{1,0:T(4,128)S(1)} %add.184) | copy-start | bytes 2308
  3.7 5.4 %copy-start.72 = (f32[3,64]{1,0:T(4,128)}, f32[3,64]{1,0:T(4,128)S(1)}, u32[]{:S(2)}) copy-start(f32[3,64]{1,0:T(4,128)S(1)} %add.168) | copy-start | bytes 2308
  3.8 6.1 %copy-start.81 = (f32[3,64]{1,0:T(4,128)}, f32[3,64]{1,0:T(4,128)S(1)}, u32[]{:S(2)}) copy-start(f32[3,64]{1,0:T(4,128)S(1)} %add.165) | copy-start | bytes 2308
  3.8 46.6 %copy-start.76 = (f32[3,64]{1,0:T(4,128)}, f32[3,64]{1,0:T(4,128)S(1)}, u32[]{:S(2)}) copy-start(f32[3,64]{1,0:T(4,128)S(1)} %add.187) | copy-start | bytes 2308
  4.5 21.6 %copy-start.60 = (f32[768]{0:T(1024)}, f32[768]{0:T(1024)S(1)}, u32[]{:S(2)}) copy-start(f32[768]{0:T(1024)S(1)} %get-tuple-element.116) | copy-start | bytes 9220
  4.6 21.6 %copy-start.89 = (f32[768]{0:T(1024)}, f32[768]{0:T(1024)S(1)}, u32[]{:S(2)}) copy-start(f32[768]{0:T(1024)S(1)} %get-tuple-element.69) | copy-start | bytes 9220
  4.6 41.3 %copy-start.91 = (f32[768]{0:T(1024)}, f32[768]{0:T(1024)S(1)}, u32[]{:S(2)}) copy-start(f32[768]{0:T(1024)S(1)} %get-tuple-element.68) | copy-start | bytes 9220
  11.1 14.6 %copy-start.50 = (bf16[394,192]{0,1:T(8,128)(2,1)}, bf16[394,192]{0,1:T(8,128)(2,1)S(1)}, u32[]{:S(2)}) copy-start(bf16[394,192]{0,1:T(8,128)(2,1)S(1)} %convert_element_type.213) | copy-start | bytes 453892
  53.4 15.0 %copy-start.52 = (bf16[394,192]{0,1:T(8,128)(2,1)}, bf16[394,192]{0,1:T(8,128)(2,1)S(1)}, u32[]{:S(2)}) copy-start(bf16[394,192]{0,1:T(8,128)(2,1)S(1)} %convert_element_type.227) | copy-start | bytes 453892
  53.4 15.0 %copy-start.32 = (f32[394,768]{1,0:T(8,128)S(1)}, f32[394,768]{1,0:T(8,128)}, u32[]{:S(2)}) copy-start(f32[394,768]{1,0:T(8,128)} %copy-done.31) | copy-start | bytes 3631108
  79.2 37.0 %copy-start.22 = (f32[394,1]{1,0:T(8,128)S(1)}, f32[394,1]{1,0:T(8,128)}, u32[]{:S(2)}) copy-start(f32[394,1]{1,0:T(8,128)} %copy-done.21) | copy-start | bytes 4732
  135.1 32.1 %copy-start.2 = (bf16[394,768]{1,0:T(8,128)(2,1)S(1)}, bf16[394,768]{1,0:T(8,128)(2,1)}, u32[]{:S(2)}) copy-start(bf16[394,768]{1,0:T(8,128)(2,1)} %cotangent_ref.3) | copy-start | bytes 1815556
  135.1 32.1 %copy-start.24 = (s32[394,2]{1,0:T(8,128)S(1)}, s32[394,2]{1,0:T(8,128)}, u32[]{:S(2)}) copy-start(s32[394,2]{1,0:T(8,128)} %copy-done.23) | copy-start | bytes 9460
  209.1 13.7 %copy-start.63 = (f32[394]{0:T(512)S(1)}, f32[394]{0:T(512)}, u32[]{:S(2)}) copy-start(f32[394]{0:T(512)} %copy-done.62) | copy-start | bytes 4732
  209.1 13.7 %copy-start.69 = (f32[394]{0:T(512)S(1)}, f32[394]{0:T(512)}, u32[]{:S(2)}) copy-start(f32[394]{0:T(512)} %copy-done.68) | copy-start | bytes 4732
  232.7 13.8 %copy-start.28 = (bf16[394,768]{1,0:T(8,128)(2,1)S(1)}, bf16[394,768]{1,0:T(8,128)(2,1)}, u32[]{:S(2)}) copy-start(bf16[394,768]{1,0:T(8,128)(2,1)} %param.14) | copy-start | bytes 1815556
  232.7 13.7 %copy-start.61 = (f32[768]{0:T(1024)S(1)}, f32[768]{0:T(1024)}, u32[]{:S(2)}) copy-start(f32[768]{0:T(1024)} %copy-done.60) | copy-start | bytes 9220
  232.7 13.7 %copy-start.67 = (f32[394]{0:T(512)S(1)}, f32[394]{0:T(512)}, u32[]{:S(2)}) copy-start(f32[394]{0:T(512)} %copy-done.66) | copy-start | bytes 4732
  232.7 13.7 %copy-start.75 = (f32[394]{0:T(512)S(1)}, f32[394]{0:T(512)}, u32[]{:S(2)}) copy-start(f32[394]{0:T(512)} %copy-done.74) | copy-start | bytes 4732
  262.2 13.7 %copy-start.59 = (f32[768]{0:T(1024)S(1)}, f32[768]{0:T(1024)}, u32[]{:S(2)}) copy-start(f32[768]{0:T(1024)} %copy-done.58) | copy-start | bytes 9220
  262.2 13.7 %copy-start.65 = (f32[394]{0:T(512)S(1)}, f32[394]{0:T(512)}, u32[]{:S(2)}) copy-start(f32[394]{0:T(512)} %copy-done.64) | copy-start | bytes 4732
  262.2 13.7 %copy-start.71 = (f32[394]{0:T(512)S(1)}, f32[394]{0:T(512)}, u32[]{:S(2)}) copy-start(f32[394]{0:T(512)} %copy-done.70) | copy-start | bytes 4732
  (77 other events, 145.5 us)
